TPU v7x, 512 devices: a whole 4x8x8 slice. The times are simulated.
512 devices in a mesh: gx: 8 (over y), gy: 8 (over x, core), gz: 8 (over z).
Axes of the slice: x: 4, y: 8, z: 8, core: 2. Of those that a mesh axis runs over, the one named last changes fastest.
Arguments:
- offsets: float32 [3, 16, 16, 16, 128], P(None, 'gx', 'gy', 'gz'), may hold values from -0.5 to 0.5
- lines: float32 [3, 16, 16, 16, 128], P(None, 'gx', 'gy', 'gz'), may hold values from -4 to 4
- burgers: float32 [3, 16, 16, 16, 128], P(None, 'gx', 'gy', 'gz'), may hold values from -4 to 4
- counts: int32 [16, 16, 16], P('gx', 'gy', 'gz'), may hold values from 64 to 128, as said below
- mobility: float32 [16, 16, 16], P('gx', 'gy', 'gz'), may hold values from 0.5 to 2
- stress: float32 [3, 3], replicated, may hold values from -3 to 3
- translation: float32 [128, 128], replicated, may hold values from -0.625 to 0.625
Outputs:
- velocity: float32 [3, 16, 16, 16, 128], P(None, 'gx', 'gy', 'gz')
Inputs may be any that keep to these rules, and one draw needn't show every extreme that they name: `counts`: some cell holds 128 live segments.
All inputs are finite; a program needn't handle non-finite values.
Results may differ from a plain program's by a relative error of at most 0.0003.
Values sent between devices are 32-bit elements; how exact they have to be, the bound alone decides.
A program may use at most 64 MiB of HBM per device.

v0:
```python
import jax
import jax.numpy as jnp
from jax import lax
from jax.sharding import PartitionSpec as P

core_square = 0.0625
near_scale = 0.01
highest = lax.Precision.HIGHEST


def padded_2(value, sides, width):
    for axis, dim in sides:
        count, length = (lax.axis_size(axis), value.shape[dim])
        up = [(i, (i + 1) % count) for i in range(count)]
        down = [(j, i) for i, j in up]
        last = lax.slice_in_dim(value, length - width, length, axis=dim)
        first = lax.slice_in_dim(value, 0, width, axis=dim)
        before = lax.ppermute(last, axis, up)
        after = lax.ppermute(first, axis, down)
        value = jnp.concatenate([before, value, after], axis=dim)
    return value


def exponent_list():
    result = []
    for first in range(5):
        for second in range(5 - first):
            for third in range(5 - first - second):
                result.append((first, second, third))
    return result


def monomials(relative):
    powers = []
    for column in range(3):
        base = relative[column]
        square = base * base
        powers.append([jnp.ones_like(base), base, square, square * base, square * square])
    return jnp.stack(
        [
            powers[0][first] * powers[1][second] * powers[2][third]
            for first, second, third in exponent_list()
        ]
    )


def crossed(left, right):
    return jnp.stack(
        [
            left[1] * right[2] - left[2] * right[1],
            left[2] * right[0] - left[0] * right[2],
            left[0] * right[1] - left[1] * right[0],
        ]
    )


def pair_forces(target, source, shift):
    separation = [
        shift[column] + source[column][..., None, :] - target[column][..., :, None]
        for column in range(3)
    ]
    radius_sq = (
        separation[0] * separation[0]
        + separation[1] * separation[1]
        + separation[2] * separation[2]
        + core_square
    )
    inverse = 1.0 / (radius_sq * jnp.sqrt(radius_sq))
    burgers_dot = sum(
        (target[6 + column][..., :, None] * source[6 + column][..., None, :] for column in range(3))
    )
    line_dot = sum(
        (target[3 + column][..., :, None] * source[3 + column][..., None, :] for column in range(3))
    )
    target_proj = sum(
        (target[6 + column][..., :, None] * separation[column] for column in range(3))
    )
    source_proj = sum(
        (source[6 + column][..., None, :] * separation[column] for column in range(3))
    )
    first_coef = inverse * burgers_dot * line_dot
    second_coef = inverse * target_proj * source_proj / radius_sq
    return jnp.stack(
        [
            jnp.sum(
                first_coef * separation[column] + second_coef * source[3 + column][..., None, :], -1
            )
            for column in range(3)
        ]
    )


def near_total(inner, padded):
    extent = inner.shape[1:4]
    total = jnp.zeros((3,) + inner.shape[1:], jnp.float32)
    for step_x in (-1, 0, 1):
        for step_y in (-1, 0, 1):
            for step_z in (-1, 0, 1):
                source = padded[
                    :,
                    1 + step_x : 1 + step_x + extent[0],
                    1 + step_y : 1 + step_y + extent[1],
                    1 + step_z : 1 + step_z + extent[2],
                ]
                total = total + pair_forces(
                    inner, source, (float(step_x), float(step_y), float(step_z))
                )
    return near_scale * total


def cell_moments(poly, charge, slots, width):
    moments = jnp.einsum("kxyzs,cxyzs->xyzck", poly, charge, precision=highest) / slots
    flat = moments.reshape(-1, 3 * poly.shape[0])
    return jnp.pad(flat, ((0, 0), (0, width - flat.shape[1])))


def far_weights(rows_first, rows_second, extents):
    total_sq = jnp.zeros((rows_first[0].shape[0], rows_second[0].shape[0]), jnp.float32)
    largest = jnp.zeros((rows_first[0].shape[0], rows_second[0].shape[0]), jnp.int32)
    for column in range(3):
        spacing = (
            jnp.abs(rows_first[column][:, None] - rows_second[column][None, :]) % extents[column]
        )
        spacing = jnp.minimum(spacing, extents[column] - spacing)
        largest = jnp.maximum(largest, spacing)
        total_sq = total_sq + spacing.astype(jnp.float32) * spacing.astype(jnp.float32)
    return jnp.where(largest > 1, 1.0 / jnp.sqrt(jnp.maximum(total_sq, 1.0)), 0.0)


def finish(lines, charge, mask, poly, near, coefficients, mobility, stress):
    terms = poly.shape[0]
    blocks = coefficients[..., : 3 * terms].reshape(coefficients.shape[:3] + (3, terms))
    far = jnp.einsum("kxyzs,xyzak->axyzs", poly, blocks, precision=highest)
    stressed = jnp.stack(
        [sum((stress[row, column] * charge[column] for column in range(3))) for row in range(3)]
    )
    applied = crossed(stressed, lines)
    force = near + far * mask + applied
    along = jnp.sum(force * lines, 0) / jnp.maximum(jnp.sum(lines * lines, 0), 1.0)
    return mobility[..., None] * mask * (force - along * lines)


def body(offsets, lines, burgers, counts, mobility, stress, translation):
    slots = offsets.shape[-1]
    edge = offsets.shape[1:4]
    mask = (lax.broadcasted_iota(jnp.int32, counts.shape + (slots,), 3) < counts[..., None]).astype(
        jnp.float32
    )
    charge = burgers * mask
    stacked = jnp.concatenate([offsets, lines, charge], 0)
    padded = padded_2(stacked, (("gx", 1), ("gy", 2), ("gz", 3)), 1)
    poly = monomials(offsets)
    moments = cell_moments(poly, crossed(charge, lines), slots, translation.shape[0])
    devices_along = (lax.axis_size("gx"), lax.axis_size("gy"), lax.axis_size("gz"))
    extents = (edge[0] * devices_along[0], edge[1] * devices_along[1], edge[2] * devices_along[2])
    local_cells = edge[0] * edge[1] * edge[2]
    local_index = jnp.arange(local_cells, dtype=jnp.int32)
    mine = (
        lax.axis_index("gx") * edge[0] + local_index // (edge[1] * edge[2]),
        lax.axis_index("gy") * edge[1] + local_index // edge[2] % edge[1],
        lax.axis_index("gz") * edge[2] + local_index % edge[2],
    )
    piece = lax.all_gather(moments, ("gx", "gy", "gz"), axis=0, tiled=True)
    rows = jnp.arange(piece.shape[0], dtype=jnp.int32)
    device = rows // local_cells
    within = rows % local_cells
    weights = far_weights(
        mine,
        (
            device // (devices_along[1] * devices_along[2]) * edge[0]
            + within // (edge[1] * edge[2]),
            device // devices_along[2] % devices_along[1] * edge[1] + within // edge[2] % edge[1],
            device % devices_along[2] * edge[2] + within % edge[2],
        ),
        extents,
    )
    local = jnp.dot(weights, piece, precision=highest, preferred_element_type=jnp.float32)
    near = near_total(stacked, padded)
    coefficients = jnp.dot(
        local, translation, precision=highest, preferred_element_type=jnp.float32
    )
    coefficients = coefficients.reshape(edge[0], edge[1], edge[2], -1)
    return finish(lines, charge, mask, poly, near, coefficients, mobility, stress)


def solution(mesh):
    placed = (
        P(None, "gx", "gy", "gz", None),
        P(None, "gx", "gy", "gz", None),
        P(None, "gx", "gy", "gz", None),
        P("gx", "gy", "gz"),
        P("gx", "gy", "gz"),
        P(),
        P(),
    )
    return jax.shard_map(
        body, mesh=mesh, in_specs=placed, out_specs=P(None, "gx", "gy", "gz", None), check_vma=False
    )
```

profile of v0, /device:TPU:1, one launch (start us, length us, event | category | flops | bytes accessed | tf_op | source)
XLA Modules:
  0.0 184.5 jit_solution(2565646264809706676)
XLA Ops:
  8.8 4.0 %collective-permute-start = (f32[9,1,2,2,128]{4,3,2,1,0:T(2,128)S(1)}, f32[9,1,2,2,128]{4,3,2,1,0:T(2,128)S(1)}, u32[]{:S(2)}, u32[]{:S(2)}) collective-permute-start(f32[9,1,2,2,128]{4,3,2,1,0:T(2,128)S(1)} %get-tuple-element.336), channel_id=1, source_target_pairs={{0,64},{64,128},{128,192},{192,256},{256,320},{320,384},{384,448},... | collective-permute-start | bytes 55304 | tf_op jit(solution)/shard_map/ppermute | solution.py:18
  12.8 3.8 %collective-permute-start.1 = (f32[9,1,2,2,128]{4,3,2,1,0:T(2,128)S(1)}, f32[9,1,2,2,128]{4,3,2,1,0:T(2,128)S(1)}, u32[]{:S(2)}, u32[]{:S(2)}) collective-permute-start(f32[9,1,2,2,128]{4,3,2,1,0:T(2,128)S(1)} %get-tuple-element.337), channel_id=1, source_target_pairs={{64,0},{128,64},{192,128},{256,192},{320,256},{384,320},{448,384},... | collective-permute-start | bytes 55304 | tf_op jit(solution)/shard_map/ppermute | solution.py:19
  29.1 4.5 %multiply_subtract_fusion.2 = (f32[1,2,2,2,128]{4,3,2,1,0:T(2,128)S(1)}, f32[1,2,2,2,128]{4,3,2,1,0:T(2,128)S(1)}, f32[1,2,2,2,128]{4,3,2,1,0:T(2,128)S(1)}, f32...) fusion(f32[3,2,2,2,128]{4,3,2,1,0:T(2,128)} %param.8, ...), kind=kLoop, calls=%fused_computation.1321 | loop fusion | flops 16384 | bytes 53272 | tf_op jit(solution)/shard_map/sub | solution.py:50
  33.5 2.6 %multiply_subtract_fusion.1 = (f32[1,2,2,2,128]{4,3,2,1,0:T(2,128)S(1)}, f32[1,2,2,2,128]{4,3,2,1,0:T(2,128)S(1)}) fusion(f32[1,2,2,2,128]{4,3,2,1,0:T(2,128)S(1)} %get-tuple-element.90, f32[3,2,2,2,128]{4,3,2,1,0:T(2,128)} %param.8, f32[3,2,2,2,128]{4,3,2,1,0:T(2,128)S(1)} %broadcast_multiply_fusion, f32[]{:T(128)} %bitcast.334, f32[]{:T(128)} %bitcast.333, ...), kind=kLoop, calls=%fused_computation.1319 | loop fusion | flops 8192 | bytes 32780 | tf_op jit(solution)/shard_map/sub | solution.py:51
  53.4 6.1 %collective-permute-start.3 = (f32[9,4,1,2,128]{4,3,2,1,0:T(2,128)S(1)}, f32[9,4,1,2,128]{4,3,2,1,0:T(2,128)S(1)}, u32[]{:S(2)}, u32[]{:S(2)}) collective-permute-start(f32[9,4,1,2,128]{4,3,2,1,0:T(2,128)S(1)} %get-tuple-element.317), channel_id=1, source_target_pairs={{8,0},{16,8},{24,16},{32,24},{40,32},{48,40},{56,48},{0,56},{9,1},... | collective-permute-start | bytes 110600 | tf_op jit(solution)/shard_map/ppermute | solution.py:19
  61.8 2.2 %fusion.95 = (f32[2,2,2,128]{3,2,1,0:T(2,128)S(1)}, f32[2,2,2,128]{3,2,1,0:T(2,128)S(1)}, f32[2,2,2,128]{3,2,1,0:T(2,128)S(1)}) fusion(f32[2,2,2,128]{3,2,1,0:T(2,128)S(1)} %get-tuple-element.319, f32[2,2,2,128]{3,2,1,0:T(2,128)S(1)} %get-tuple-element.334, f32[2,2,2,128]{3,2,1,0:T(2,128)S(1)} %get-tuple-element.342, ...), kind=kLoop, calls=%fused_computation.447 | loop fusion | flops 6288384 | bytes 86016 | tf_op jit(solution)/shard_map/reduce_sum | solution.py:85
  66.3 6.8 %collective-permute-start.5 = (f32[9,4,4,1,128]{4,3,2,1,0:T(1,128)S(1)}, f32[9,4,4,1,128]{4,3,2,1,0:T(1,128)S(1)}, u32[]{:S(2)}, u32[]{:S(2)}) collective-permute-start(f32[9,4,4,1,128]{4,3,2,1,0:T(1,128)S(1)} %get-tuple-element.259), channel_id=1, source_target_pairs={{1,0},{2,1},{3,2},{4,3},{5,4},{6,5},{7,6},{0,7},{9,8},{10,9},{11,1... | collective-permute-start | bytes 221192 | tf_op jit(solution)/shard_map/ppermute | solution.py:19
  73.2 2.2 %fusion.431 = (f32[2,2,2,128]{3,2,1,0:T(2,128)S(1)}, f32[2,2,2,128]{3,2,1,0:T(2,128)S(1)}, f32[2,2,2,128]{3,2,1,0:T(2,128)S(1)}) fusion(f32[2,2,2,128]{3,2,1,0:T(2,128)S(1)} %get-tuple-element.290, f32[2,2,2,128]{3,2,1,0:T(2,128)S(1)} %get-tuple-element.296, f32[2,2,2,128]{3,2,1,0:T(2,128)S(1)} %get-tuple-element.342, ...), kind=kLoop, calls=%fused_computation.783 | loop fusion | flops 6288384 | bytes 86016 | tf_op jit(solution)/shard_map/reduce_sum | solution.py:85
  75.4 2.2 %fusion.335 = (f32[2,2,2,128]{3,2,1,0:T(2,128)S(1)}, f32[2,2,2,128]{3,2,1,0:T(2,128)S(1)}, f32[2,2,2,128]{3,2,1,0:T(2,128)S(1)}) fusion(f32[2,2,2,128]{3,2,1,0:T(2,128)S(1)} %get-tuple-element.263, f32[2,2,2,128]{3,2,1,0:T(2,128)S(1)} %get-tuple-element.269, f32[2,2,2,128]{3,2,1,0:T(2,128)S(1)} %get-tuple-element.342, ...), kind=kLoop, calls=%fused_computation.687 | loop fusion | flops 6288384 | bytes 86016 | tf_op jit(solution)/shard_map/reduce_sum | solution.py:85
  77.7 2.2 %fusion.287 = (f32[2,2,2,128]{3,2,1,0:T(2,128)S(1)}, f32[2,2,2,128]{3,2,1,0:T(2,128)S(1)}, f32[2,2,2,128]{3,2,1,0:T(2,128)S(1)}) fusion(f32[2,2,2,128]{3,2,1,0:T(2,128)S(1)} %get-tuple-element.299, f32[2,2,2,128]{3,2,1,0:T(2,128)S(1)} %get-tuple-element.305, f32[2,2,2,128]{3,2,1,0:T(2,128)S(1)} %get-tuple-element.342, ...), kind=kLoop, calls=%fused_computation.639 | loop fusion | flops 6288384 | bytes 86016 | tf_op jit(solution)/shard_map/reduce_sum | solution.py:85
  79.9 2.2 %fusion.191 = (f32[2,2,2,128]{3,2,1,0:T(2,128)S(1)}, f32[2,2,2,128]{3,2,1,0:T(2,128)S(1)}, f32[2,2,2,128]{3,2,1,0:T(2,128)S(1)}) fusion(f32[2,2,2,128]{3,2,1,0:T(2,128)S(1)} %get-tuple-element.272, f32[2,2,2,128]{3,2,1,0:T(2,128)S(1)} %get-tuple-element.278, f32[2,2,2,128]{3,2,1,0:T(2,128)S(1)} %get-tuple-element.342, ...), kind=kLoop, calls=%fused_computation.543 | loop fusion | flops 6288384 | bytes 86016 | tf_op jit(solution)/shard_map/reduce_sum | solution.py:85
  82.1 2.2 %fusion.143 = (f32[2,2,2,128]{3,2,1,0:T(2,128)S(1)}, f32[2,2,2,128]{3,2,1,0:T(2,128)S(1)}, f32[2,2,2,128]{3,2,1,0:T(2,128)S(1)}) fusion(f32[2,2,2,128]{3,2,1,0:T(2,128)S(1)} %get-tuple-element.307, f32[2,2,2,128]{3,2,1,0:T(2,128)S(1)} %get-tuple-element.313, f32[2,2,2,128]{3,2,1,0:T(2,128)S(1)} %get-tuple-element.342, ...), kind=kLoop, calls=%fused_computation.495 | loop fusion | flops 6288384 | bytes 86016 | tf_op jit(solution)/shard_map/reduce_sum | solution.py:85
  84.4 2.2 %fusion.47 = (f32[2,2,2,128]{3,2,1,0:T(2,128)S(1)}, f32[2,2,2,128]{3,2,1,0:T(2,128)S(1)}, f32[2,2,2,128]{3,2,1,0:T(2,128)S(1)}) fusion(f32[2,2,2,128]{3,2,1,0:T(2,128)S(1)} %get-tuple-element.380, f32[2,2,2,128]{3,2,1,0:T(2,128)S(1)} %get-tuple-element.374, f32[2,2,2,128]{3,2,1,0:T(2,128)S(1)} %get-tuple-element.342, ...), kind=kLoop, calls=%fused_computation.399 | loop fusion | flops 6288384 | bytes 86016 | tf_op jit(solution)/shard_map/reduce_sum | solution.py:85
  87.3 2.2 %fusion.447 = (f32[2,2,2,128]{3,2,1,0:T(2,128)S(1)}, f32[2,2,2,128]{3,2,1,0:T(2,128)S(1)}, f32[2,2,2,128]{3,2,1,0:T(2,128)S(1)}) fusion(f32[2,2,2,128]{3,2,1,0:T(2,128)S(1)} %get-tuple-element.97, f32[2,2,2,128]{3,2,1,0:T(2,128)S(1)} %get-tuple-element.103, f32[2,2,2,128]{3,2,1,0:T(2,128)S(1)} %get-tuple-element.342, ...), kind=kLoop, calls=%fused_computation.799 | loop fusion | flops 6288384 | bytes 86016 | tf_op jit(solution)/shard_map/reduce_sum | solution.py:85
  89.5 2.2 %fusion.415 = (f32[2,2,2,128]{3,2,1,0:T(2,128)S(1)}, f32[2,2,2,128]{3,2,1,0:T(2,128)S(1)}, f32[2,2,2,128]{3,2,1,0:T(2,128)S(1)}) fusion(f32[2,2,2,128]{3,2,1,0:T(2,128)S(1)} %get-tuple-element.178, f32[2,2,2,128]{3,2,1,0:T(2,128)S(1)} %get-tuple-element.184, f32[2,2,2,128]{3,2,1,0:T(2,128)S(1)} %get-tuple-element.342, ...), kind=kLoop, calls=%fused_computation.767 | loop fusion | flops 6288384 | bytes 86016 | tf_op jit(solution)/shard_map/reduce_sum | solution.py:85
  91.8 2.2 %fusion.399 = (f32[2,2,2,128]{3,2,1,0:T(2,128)S(1)}, f32[2,2,2,128]{3,2,1,0:T(2,128)S(1)}, f32[2,2,2,128]{3,2,1,0:T(2,128)S(1)}) fusion(f32[2,2,2,128]{3,2,1,0:T(2,128)S(1)} %get-tuple-element.106, f32[2,2,2,128]{3,2,1,0:T(2,128)S(1)} %get-tuple-element.112, f32[2,2,2,128]{3,2,1,0:T(2,128)S(1)} %get-tuple-element.342, ...), kind=kLoop, calls=%fused_computation.751 | loop fusion | flops 6288384 | bytes 86016 | tf_op jit(solution)/shard_map/reduce_sum | solution.py:85
  94.0 2.2 %fusion.367 = (f32[2,2,2,128]{3,2,1,0:T(2,128)S(1)}, f32[2,2,2,128]{3,2,1,0:T(2,128)S(1)}, f32[2,2,2,128]{3,2,1,0:T(2,128)S(1)}) fusion(f32[2,2,2,128]{3,2,1,0:T(2,128)S(1)} %get-tuple-element.187, f32[2,2,2,128]{3,2,1,0:T(2,128)S(1)} %get-tuple-element.193, f32[2,2,2,128]{3,2,1,0:T(2,128)S(1)} %get-tuple-element.342, ...), kind=kLoop, calls=%fused_computation.719 | loop fusion | flops 6288384 | bytes 86016 | tf_op jit(solution)/shard_map/reduce_sum | solution.py:85
  96.3 2.2 %fusion.351 = (f32[2,2,2,128]{3,2,1,0:T(2,128)S(1)}, f32[2,2,2,128]{3,2,1,0:T(2,128)S(1)}, f32[2,2,2,128]{3,2,1,0:T(2,128)S(1)}) fusion(f32[2,2,2,128]{3,2,1,0:T(2,128)S(1)} %get-tuple-element.116, f32[2,2,2,128]{3,2,1,0:T(2,128)S(1)} %get-tuple-element.122, f32[2,2,2,128]{3,2,1,0:T(2,128)S(1)} %get-tuple-element.342, ...), kind=kLoop, calls=%fused_computation.703 | loop fusion | flops 6288384 | bytes 86016 | tf_op jit(solution)/shard_map/reduce_sum | solution.py:85
  98.5 2.2 %fusion.319 = (f32[2,2,2,128]{3,2,1,0:T(2,128)S(1)}, f32[2,2,2,128]{3,2,1,0:T(2,128)S(1)}, f32[2,2,2,128]{3,2,1,0:T(2,128)S(1)}) fusion(f32[2,2,2,128]{3,2,1,0:T(2,128)S(1)} %get-tuple-element.197, f32[2,2,2,128]{3,2,1,0:T(2,128)S(1)} %get-tuple-element.203, f32[2,2,2,128]{3,2,1,0:T(2,128)S(1)} %get-tuple-element.342, ...), kind=kLoop, calls=%fused_computation.671 | loop fusion | flops 6288384 | bytes 86016 | tf_op jit(solution)/shard_map/reduce_sum | solution.py:85
  100.7 2.2 %fusion.303 = (f32[2,2,2,128]{3,2,1,0:T(2,128)S(1)}, f32[2,2,2,128]{3,2,1,0:T(2,128)S(1)}, f32[2,2,2,128]{3,2,1,0:T(2,128)S(1)}) fusion(f32[2,2,2,128]{3,2,1,0:T(2,128)S(1)} %get-tuple-element.125, f32[2,2,2,128]{3,2,1,0:T(2,128)S(1)} %get-tuple-element.131, f32[2,2,2,128]{3,2,1,0:T(2,128)S(1)} %get-tuple-element.342, ...), kind=kLoop, calls=%fused_computation.655 | loop fusion | flops 6288384 | bytes 86016 | tf_op jit(solution)/shard_map/reduce_sum | solution.py:85
  103.0 2.2 %fusion.271 = (f32[2,2,2,128]{3,2,1,0:T(2,128)S(1)}, f32[2,2,2,128]{3,2,1,0:T(2,128)S(1)}, f32[2,2,2,128]{3,2,1,0:T(2,128)S(1)}) fusion(f32[2,2,2,128]{3,2,1,0:T(2,128)S(1)} %get-tuple-element.206, f32[2,2,2,128]{3,2,1,0:T(2,128)S(1)} %get-tuple-element.212, f32[2,2,2,128]{3,2,1,0:T(2,128)S(1)} %get-tuple-element.342, ...), kind=kLoop, calls=%fused_computation.623 | loop fusion | flops 6288384 | bytes 86016 | tf_op jit(solution)/shard_map/reduce_sum | solution.py:85
  105.2 2.2 %fusion.255 = (f32[2,2,2,128]{3,2,1,0:T(2,128)S(1)}, f32[2,2,2,128]{3,2,1,0:T(2,128)S(1)}, f32[2,2,2,128]{3,2,1,0:T(2,128)S(1)}) fusion(f32[2,2,2,128]{3,2,1,0:T(2,128)S(1)} %get-tuple-element.135, f32[2,2,2,128]{3,2,1,0:T(2,128)S(1)} %get-tuple-element.141, f32[2,2,2,128]{3,2,1,0:T(2,128)S(1)} %get-tuple-element.342, ...), kind=kLoop, calls=%fused_computation.607 | loop fusion | flops 6288384 | bytes 86016 | tf_op jit(solution)/shard_map/reduce_sum | solution.py:85
  107.4 2.2 %fusion.223 = (f32[2,2,2,128]{3,2,1,0:T(2,128)S(1)}, f32[2,2,2,128]{3,2,1,0:T(2,128)S(1)}, f32[2,2,2,128]{3,2,1,0:T(2,128)S(1)}) fusion(f32[2,2,2,128]{3,2,1,0:T(2,128)S(1)} %get-tuple-element.216, f32[2,2,2,128]{3,2,1,0:T(2,128)S(1)} %get-tuple-element.222, f32[2,2,2,128]{3,2,1,0:T(2,128)S(1)} %get-tuple-element.342, ...), kind=kLoop, calls=%fused_computation.575 | loop fusion | flops 6288384 | bytes 86016 | tf_op jit(solution)/shard_map/reduce_sum | solution.py:85
  109.7 2.2 %fusion.207 = (f32[2,2,2,128]{3,2,1,0:T(2,128)S(1)}, f32[2,2,2,128]{3,2,1,0:T(2,128)S(1)}, f32[2,2,2,128]{3,2,1,0:T(2,128)S(1)}) fusion(f32[2,2,2,128]{3,2,1,0:T(2,128)S(1)} %get-tuple-element.144, f32[2,2,2,128]{3,2,1,0:T(2,128)S(1)} %get-tuple-element.150, f32[2,2,2,128]{3,2,1,0:T(2,128)S(1)} %get-tuple-element.342, ...), kind=kLoop, calls=%fused_computation.559 | loop fusion | flops 6288384 | bytes 86016 | tf_op jit(solution)/shard_map/reduce_sum | solution.py:85
  111.9 2.2 %fusion.175 = (f32[2,2,2,128]{3,2,1,0:T(2,128)S(1)}, f32[2,2,2,128]{3,2,1,0:T(2,128)S(1)}, f32[2,2,2,128]{3,2,1,0:T(2,128)S(1)}) fusion(f32[2,2,2,128]{3,2,1,0:T(2,128)S(1)} %get-tuple-element.225, f32[2,2,2,128]{3,2,1,0:T(2,128)S(1)} %get-tuple-element.231, f32[2,2,2,128]{3,2,1,0:T(2,128)S(1)} %get-tuple-element.342, ...), kind=kLoop, calls=%fused_computation.527 | loop fusion | flops 6288384 | bytes 86016 | tf_op jit(solution)/shard_map/reduce_sum | solution.py:85
  114.2 2.2 %fusion.159 = (f32[2,2,2,128]{3,2,1,0:T(2,128)S(1)}, f32[2,2,2,128]{3,2,1,0:T(2,128)S(1)}, f32[2,2,2,128]{3,2,1,0:T(2,128)S(1)}) fusion(f32[2,2,2,128]{3,2,1,0:T(2,128)S(1)} %get-tuple-element.154, f32[2,2,2,128]{3,2,1,0:T(2,128)S(1)} %get-tuple-element.160, f32[2,2,2,128]{3,2,1,0:T(2,128)S(1)} %get-tuple-element.342, ...), kind=kLoop, calls=%fused_computation.511 | loop fusion | flops 6288384 | bytes 86016 | tf_op jit(solution)/shard_map/reduce_sum | solution.py:85
  116.4 2.2 %fusion.127 = (f32[2,2,2,128]{3,2,1,0:T(2,128)S(1)}, f32[2,2,2,128]{3,2,1,0:T(2,128)S(1)}, f32[2,2,2,128]{3,2,1,0:T(2,128)S(1)}) fusion(f32[2,2,2,128]{3,2,1,0:T(2,128)S(1)} %get-tuple-element.235, f32[2,2,2,128]{3,2,1,0:T(2,128)S(1)} %get-tuple-element.241, f32[2,2,2,128]{3,2,1,0:T(2,128)S(1)} %get-tuple-element.342, ...), kind=kLoop, calls=%fused_computation.479 | loop fusion | flops 6288384 | bytes 86016 | tf_op jit(solution)/shard_map/reduce_sum | solution.py:85
  118.6 2.5 %fusion.111 = (f32[2,2,2,128]{3,2,1,0:T(2,128)S(1)}, f32[2,2,2,128]{3,2,1,0:T(2,128)S(1)}, f32[2,2,2,128]{3,2,1,0:T(2,128)S(1)}) fusion(f32[2,2,2,128]{3,2,1,0:T(2,128)S(1)} %get-tuple-element.163, f32[2,2,2,128]{3,2,1,0:T(2,128)S(1)} %get-tuple-element.169, f32[2,2,2,128]{3,2,1,0:T(2,128)S(1)} %get-tuple-element.342, ...), kind=kLoop, calls=%fused_computation.463 | loop fusion | flops 6288384 | bytes 86016 | tf_op jit(solution)/shard_map/reduce_sum | solution.py:85
  123.3 2.2 %fusion.63 = (f32[2,2,2,128]{3,2,1,0:T(2,128)S(1)}, f32[2,2,2,128]{3,2,1,0:T(2,128)S(1)}, f32[2,2,2,128]{3,2,1,0:T(2,128)S(1)}) fusion(f32[2,2,2,128]{3,2,1,0:T(2,128)S(1)} %get-tuple-element.171, f32[2,2,2,128]{3,2,1,0:T(2,128)S(1)} %get-tuple-element.174, f32[2,2,2,128]{3,2,1,0:T(2,128)S(1)} %get-tuple-element.342, ...), kind=kLoop, calls=%fused_computation.415 | loop fusion | flops 6288384 | bytes 86016 | tf_op jit(solution)/shard_map/reduce_sum | solution.py:85
  125.6 3.4 %fusion.31 = (f32[2,2,2,128]{3,2,1,0:T(2,128)S(1)}, f32[2,2,2,128]{3,2,1,0:T(2,128)S(1)}, f32[2,2,2,128]{3,2,1,0:T(2,128)S(1)}, f32[2,2,2,128]{3,2,1,0:T(2,128)S...) fusion(f32[2,2,2,128]{3,2,1,0:T(2,128)S(1)} %get-tuple-element.249, ...), kind=kLoop, calls=%fused_computation.383 | loop fusion | flops 12576768 | bytes 98304 | tf_op jit(solution)/shard_map/reduce_sum | solution.py:85
  129.0 44.2 %all-gather.2.cloned.1.call-done = f32[4096,128]{1,0:T(8,128)} async-done(((f32[8,128]{1,0:T(8,128)}), f32[4096,128]{1,0:T(8,128)}) %all-gather.2.cloned.1.call-update) | async-done | bytes 2097168 | tf_op jit(solution)/shard_map/all_gather | solution.py:163
  173.2 3.0 %fusion.465 = f32[8,128]{1,0:T(8,128)S(1)} fusion(f32[4096,128]{1,0:T(8,128)} %all-gather.2.cloned.1.call-done, s32[4096]{0:T(1024)S(1)} %fusion.515, s32[8]{0:T(128)S(1)} %get-tuple-element.367, s32[4096]{0:T(1024)S(1)} %get-tuple-element.366, s32[8]{0:T(128)S(1)} %fusion.612, s32[4096]{0:T(1024)S(1)} %get-tuple-element.365, s32[8]{0:T(128)S(1)} %get-tuple-element.368), kind=kOutput, calls=%fused_computation.859 | convolution fusion | flops 52264960 | bytes 2150496 | tf_op jit(solution)/shard_map/dot_general | solution.py:177
  (92 shorter events, 40.6 us)
Async XLA Ops:
  6.5 169.7 %copy-start = (f32[128,128]{1,0:T(8,128)S(1)}, f32[128,128]{1,0:T(8,128)}, u32[]{:S(2)}) copy-start(f32[128,128]{1,0:T(8,128)} %param.13) | copy-start | bytes 196612
  6.5 57.5 %copy-start.2 = (f32[3,2,2,2,128]{4,3,2,1,0:T(2,128)S(1)}, f32[3,2,2,2,128]{4,3,2,1,0:T(2,128)}, u32[]{:S(2)}) copy-start(f32[3,2,2,2,128]{4,3,2,1,0:T(2,128)} %param.8) | copy-start | bytes 36868
  6.5 57.5 %copy-start.1 = (f32[3,2,2,2,128]{4,3,2,1,0:T(2,128)S(1)}, f32[3,2,2,2,128]{4,3,2,1,0:T(2,128)}, u32[]{:S(2)}) copy-start(f32[3,2,2,2,128]{4,3,2,1,0:T(2,128)} %param.7) | copy-start | bytes 36868
  6.5 166.6 %all-gather.2.cloned.1.call-start = ((), (), s32[]{:S(2)}) async-start(), calls=%async_computation | async-start | bytes 2101248 | tf_op jit(solution)/shard_map/all_gather | solution.py:163
  8.8 28.1 %collective-permute-start = (f32[9,1,2,2,128]{4,3,2,1,0:T(2,128)S(1)}, f32[9,1,2,2,128]{4,3,2,1,0:T(2,128)S(1)}, u32[]{:S(2)}, u32[]{:S(2)}) collective-permute-start(f32[9,1,2,2,128]{4,3,2,1,0:T(2,128)S(1)} %get-tuple-element.336), channel_id=1, source_target_pairs={{0,64},{64,128},{128,192},{192,256},{256,320},{320,384},{384,448},... | collective-permute-start | bytes 55304 | tf_op jit(solution)/shard_map/ppermute | solution.py:18
  12.8 35.6 %collective-permute-start.1 = (f32[9,1,2,2,128]{4,3,2,1,0:T(2,128)S(1)}, f32[9,1,2,2,128]{4,3,2,1,0:T(2,128)S(1)}, u32[]{:S(2)}, u32[]{:S(2)}) collective-permute-start(f32[9,1,2,2,128]{4,3,2,1,0:T(2,128)S(1)} %get-tuple-element.337), channel_id=1, source_target_pairs={{64,0},{128,64},{192,128},{256,192},{320,256},{384,320},{448,384},... | collective-permute-start | bytes 55304 | tf_op jit(solution)/shard_map/ppermute | solution.py:19
  53.4 10.5 %collective-permute-start.3 = (f32[9,4,1,2,128]{4,3,2,1,0:T(2,128)S(1)}, f32[9,4,1,2,128]{4,3,2,1,0:T(2,128)S(1)}, u32[]{:S(2)}, u32[]{:S(2)}) collective-permute-start(f32[9,4,1,2,128]{4,3,2,1,0:T(2,128)S(1)} %get-tuple-element.317), channel_id=1, source_target_pairs={{8,0},{16,8},{24,16},{32,24},{40,32},{48,40},{56,48},{0,56},{9,1},... | collective-permute-start | bytes 110600 | tf_op jit(solution)/shard_map/ppermute | solution.py:19
  59.5 4.5 %collective-permute-start.2 = (f32[9,4,1,2,128]{4,3,2,1,0:T(2,128)S(1)}, f32[9,4,1,2,128]{4,3,2,1,0:T(2,128)S(1)}, u32[]{:S(2)}, u32[]{:S(2)}) collective-permute-start(f32[9,4,1,2,128]{4,3,2,1,0:T(2,128)S(1)} %get-tuple-element.316), channel_id=1, source_target_pairs={{0,8},{8,16},{16,24},{24,32},{32,40},{40,48},{48,56},{56,0},{1,9},... | collective-permute-start | bytes 110600 | tf_op jit(solution)/shard_map/ppermute | solution.py:18
  64.4 22.2 %collective-permute-start.4 = (f32[9,4,4,1,128]{4,3,2,1,0:T(1,128)S(1)}, f32[9,4,4,1,128]{4,3,2,1,0:T(1,128)S(1)}, u32[]{:S(2)}, u32[]{:S(2)}) collective-permute-start(f32[9,4,4,1,128]{4,3,2,1,0:T(1,128)S(1)} %get-tuple-element.258), channel_id=1, source_target_pairs={{0,1},{1,2},{2,3},{3,4},{4,5},{5,6},{6,7},{7,0},{8,9},{9,10},{10,1... | collective-permute-start | bytes 221192 | tf_op jit(solution)/shard_map/ppermute | solution.py:18
  66.3 20.3 %collective-permute-start.5 = (f32[9,4,4,1,128]{4,3,2,1,0:T(1,128)S(1)}, f32[9,4,4,1,128]{4,3,2,1,0:T(1,128)S(1)}, u32[]{:S(2)}, u32[]{:S(2)}) collective-permute-start(f32[9,4,4,1,128]{4,3,2,1,0:T(1,128)S(1)} %get-tuple-element.259), channel_id=1, source_target_pairs={{1,0},{2,1},{3,2},{4,3},{5,4},{6,5},{7,6},{0,7},{9,8},{10,9},{11,1... | collective-permute-start | bytes 221192 | tf_op jit(solution)/shard_map/ppermute | solution.py:19
Sparse Core Ops, SparseCore 0:
  52.8 120.3 all-gather.1
where the time goes:
time: 187 us; the launch traced here: 184 us
  other arithmetic  96 us (51%)
  waiting for transfers between devices  44.2 us (24%)
  starting transfers between devices  22.7 us (12%)
  between operations  13.7 us (7%)
  local copies, waits for them, and re-layouts  4.04 us (2%)
  matrix products  3.82 us (2%)
    reduce_sum x26, other arithmetic, pair_forces(): jnp.sum(first_coef * separation[column] + second_coef * source[3 + column...  59.5 us
    all_gather x1, waiting for transfers between devices, body(): piece = lax.all_gather(moments, ('gx', 'gy', 'gz'), axis=0, tiled=True)  44.2 us
    unnamed x27, other arithmetic  19.2 us
    ppermute x3, starting transfers between devices, padded_2(): after = lax.ppermute(first, axis, down)  16.7 us
    ppermute x3, starting transfers between devices, padded_2(): before = lax.ppermute(last, axis, up)  5.96 us
    sub x1, other arithmetic, crossed(): left[1] * right[2] - left[2] * right[1]  4.47 us
    mul x12, other arithmetic, pair_forces(): target[3 + column][..., :, None] * source[3 + column][..., None, :]  4.01 us
  transfers between devices with their start and end apart: 7, of which 1 were waited for; matrix products, arithmetic and copies ran while one was open for 50% of the time, Pallas kernels for 0%

commit v1 on v0

v1 whole, which is shorter than its diff:
```python
import functools

import jax
import jax.numpy as jnp
from jax import lax
from jax.experimental import pallas as pl
from jax.experimental.pallas import tpu as pltpu
from jax.sharding import PartitionSpec as P

MESH = pl.DeviceIdType.MESH
core_square = 0.0625
near_scale = 0.01
slots = 128
terms = 35
term_rows = 40
source_rows = 40
split_rows = 32
f32, bf16 = jnp.float32, jnp.bfloat16

offsets_26 = [
    (x, y, z)
    for x in (-1, 0, 1)
    for y in (-1, 0, 1)
    for z in (-1, 0, 1)
    if (x, y, z) != (0, 0, 0)
]


def exponent_list():
    result = []
    for first in range(5):
        for second in range(5 - first):
            for third in range(5 - first - second):
                result.append((first, second, third))
    return result


def crossed(left, right):
    return [
        left[1] * right[2] - left[2] * right[1],
        left[2] * right[0] - left[0] * right[2],
        left[0] * right[1] - left[1] * right[0],
    ]


def high_low(value):
    high = value.astype(bf16).astype(f32)
    return high, value - high


def split_three(value):
    first, rest = high_low(value)
    second, rest = high_low(rest)
    return [first, second, rest.astype(bf16).astype(f32)]


def two_parts(value):
    high = value.astype(bf16)
    return high, (value - high.astype(f32)).astype(bf16)


def source_values(position, line, charge):
    pairs = [charge[a] * line[b] for a in range(3) for b in range(3)]
    projection = sum(charge[c] * position[c] for c in range(3))
    rows = list(pairs)
    for c in range(3):
        rows += [position[c] * value for value in pairs]
    rows += [projection * line[c] for c in range(3)]
    rows.append(jnp.zeros_like(projection))
    splits = []
    for c in range(3):
        first, second, third = split_three(position[c])
        splits += [first, first, first, second, second, third]
    splits += split_three(sum(position[c] * position[c] for c in range(3)))
    one = jnp.ones_like(projection)
    zero = jnp.zeros_like(projection)
    splits += [one] * 3 + [zero] * 8
    return rows, splits


def target_values(position, charge):
    squares = sum(position[c] * position[c] for c in range(3)) + core_square
    projection = sum(charge[c] * position[c] for c in range(3))
    zero = jnp.zeros_like(squares)
    one = jnp.ones_like(squares)
    distance, along = [], []
    for c in range(3):
        first, second, third = split_three(-2.0 * position[c])
        distance += [first, second, third, first, second, first]
        first, second, third = split_three(charge[c])
        along += [first, second, third, first, second, first]
    distance += [one] * 3 + split_three(squares) + [zero] * 8
    along += [zero] * 3 + split_three(-projection) + [zero] * 8
    return distance, along


def store_rows(ref, values, stride, first=0):
    for n, value in enumerate(values):
        ref[pl.ds(first + n, 8, stride=stride), :] = value


def eight_cells(halo, group, n):
    flat = halo.reshape(64 * 16, slots)
    return flat[pl.ds(group * 8 * 16 + n, 8, stride=16), :]


def pack_sources(stage_rows, stage_split, out_rows, out_split, first, first_split):
    for cell in range(8):
        value = stage_rows[pl.ds(cell * source_rows, source_rows), :]
        high, low = high_low(value)
        out_rows[first + cell] = jnp.concatenate([high, low], 0).astype(bf16)
    for half in range(2):
        value = stage_split[pl.ds(half * 4 * split_rows, 4 * split_rows), :]
        out_split[first_split + half] = value.T.astype(bf16)


def pair_weights(split, target):
    both = jnp.dot(split, target, preferred_element_type=f32)
    inverse = lax.rsqrt(both[:, :slots])
    square = inverse * inverse
    cube = square * inverse
    value = jnp.concatenate([cube, cube * square * both[:, slots:]], 1)
    return two_parts(value)


def summed(items):
    highs, lows, rows = [], [], []
    for split, target, row in items:
        high, low = pair_weights(split, target)
        highs.append(high)
        lows.append(low)
        rows.append(row)
    return jnp.dot(
        jnp.concatenate(rows + rows, 1),
        jnp.concatenate(highs + lows, 0),
        preferred_element_type=f32,
    )


def kernel(
    sizes,
    offsets_ref,
    lines_ref,
    burgers_ref,
    counts_ref,
    mobility_ref,
    stress_ref,
    translation_ref,
    out_ref,
    halo,
    gathered,
    partial,
    received,
    stage_rows,
    stage_split,
    stage_poly,
    local_rows,
    local_split,
    halo_rows,
    halo_split,
    target_rows,
    poly_rows,
    translation_rows,
    near_w,
    near_c,
    halo_send,
    halo_recv,
    line_send,
    line_recv,
):
    me = [lax.axis_index(name) for name in ("gx", "gy", "gz")]
    count_x, count_y, count_z = sizes

    def device(step_x, step_y, step_z):
        return tuple(
            lax.rem(me[axis] + step + sizes[axis], sizes[axis])
            for axis, step in enumerate((step_x, step_y, step_z))
        )

    partners = list(offsets_26)
    partners += [(u, 0, 0) for u in range(1, count_x) if u not in (1, count_x - 1)]
    partners += [(0, u, 0) for u in range(1, count_y) if u not in (1, count_y - 1)]
    partners += [(0, 0, u) for u in range(1, count_z) if u not in (1, count_z - 1)]
    barrier = pltpu.get_barrier_semaphore()
    for step in partners:
        pl.semaphore_signal(barrier, inc=1, device_id=device(*step), device_id_type=MESH)

    cell = lax.broadcasted_iota(jnp.int32, (8, slots), 0)
    lane = lax.broadcasted_iota(jnp.int32, (8, slots), 1)
    counts = jnp.zeros((8, slots), jnp.int32)
    mobility = jnp.zeros((8, slots), f32)
    for k in range(8):
        where = (k // 4, k // 2 % 2, k % 2)
        counts = jnp.where(cell == k, counts_ref[where], counts)
        mobility = jnp.where(cell == k, mobility_ref[where], mobility)
    mask = jnp.where(lane < counts, 1.0, 0.0).astype(f32)
    offsets = [offsets_ref[c] for c in range(3)]
    lines = [lines_ref[c] for c in range(3)]
    charge = [burgers_ref[c] * mask for c in range(3)]

    powers = []
    for base in offsets:
        square = base * base
        powers.append([jnp.ones_like(base), base, square, square * base, square * square])
    poly = []
    for first, second, third in exponent_list():
        factors = [powers[c][e] for c, e in enumerate((first, second, third)) if e]
        value = factors[0] if factors else powers[0][0]
        for factor in factors[1:]:
            value = value * factor
        poly.append(value)
    poly += [jnp.zeros((8, slots), f32)] * (term_rows - terms)
    store_rows(stage_poly, poly, term_rows)
    pad = jnp.zeros((slots - 2 * term_rows, slots), f32)
    for k in range(8):
        high, low = high_low(stage_poly[pl.ds(k * term_rows, term_rows), :])
        poly_rows[k] = jnp.concatenate([high, low, pad], 0).astype(bf16)
    dipole = crossed(charge, lines)
    highs, lows = [], []
    for value in dipole:
        high, low = high_low(value)
        highs.append(high)
        lows.append(low)
    zero = jnp.zeros((8, slots), f32)
    left = []
    for parts in (highs, lows):
        for k in range(8):
            rows = [jnp.where(cell == k, part, 0.0) for part in parts] + [zero]
            left.append(jnp.concatenate(rows, 0).astype(bf16))
    right = [poly_rows[k] for k in range(8)]
    moments = lax.dot_general(
        jnp.concatenate(left, 1),
        jnp.concatenate(right + right, 1),
        (((1,), (1,)), ((), ())),
        preferred_element_type=f32,
    )
    total = zero
    for m in range(3):
        part = moments[8 * m : 8 * m + 8]
        part = part + pltpu.roll(part, slots - term_rows, 1)
        part = jnp.where(lane < terms, part, 0.0)
        total = total + (part if m == 0 else pltpu.roll(part, terms * m, 1))
    gathered[0, 0] = total * (1.0 / slots)

    for c in range(3):
        for first, value in ((0, offsets), (3, lines), (6, charge)):
            for k in range(8):
                where = (1 + k // 4, 1 + k // 2 % 2, 1 + k % 2, pl.ds(first + c, 1))
                halo[where] = value[c][k : k + 1]

    pl.semaphore_wait(barrier, len(partners))

    def line_copy(axis, u, source, target):
        step = [0, 0, 0]
        step[axis] = u
        return pltpu.make_async_remote_copy(
            src_ref=source,
            dst_ref=target,
            send_sem=line_send.at[axis, u],
            recv_sem=line_recv.at[axis, u],
            device_id=device(*step),
            device_id_type=MESH,
        )

    copies_z = [
        line_copy(2, u, gathered.at[0, 0], gathered.at[0, u]) for u in range(1, count_z)
    ]
    for copy in copies_z:
        copy.start()
    sides = {
        -1: (pl.ds(1, 1), pl.ds(3, 1)),
        0: (pl.ds(1, 2), pl.ds(1, 2)),
        1: (pl.ds(2, 1), pl.ds(0, 1)),
    }
    copies_halo = []
    for n, step in enumerate(offsets_26):
        source = tuple(sides[s][0] for s in step)
        target = tuple(sides[s][1] for s in step)
        copies_halo.append(
            pltpu.make_async_remote_copy(
                src_ref=halo.at[source],
                dst_ref=halo.at[target],
                send_sem=halo_send.at[n],
                recv_sem=halo_recv.at[n],
                device_id=device(*step),
                device_id_type=MESH,
            )
        )
    for copy in copies_halo:
        copy.start()

    corner = [cell // 4, cell // 2 % 2, cell % 2]
    position = [offsets[c] + (corner[c].astype(f32) - 0.5) for c in range(3)]
    rows, splits = source_values(position, lines, charge)
    store_rows(stage_rows, rows, source_rows)
    store_rows(stage_split, splits, split_rows)
    pack_sources(stage_rows, stage_split, local_rows, local_split, 0, 0)
    distance, along = target_values(position, charge)
    target_rows[...] = jnp.zeros(target_rows.shape, bf16)
    for side, values in enumerate((distance, along)):
        store_rows(stage_split, values, split_rows)
        for k in range(8):
            value = stage_split[pl.ds(k * split_rows, split_rows), :].astype(bf16)
            for block in range(4):
                target_rows[
                    k, block, pl.ds(block * split_rows, split_rows), pl.ds(side * slots, slots)
                ] = value

    def near_local(k, _):
        items = []
        for source in range(8):
            items.append(
                (local_split[source // 4], target_rows[k, source % 4], local_rows[source])
            )
        value = summed(items)
        value = value[:source_rows] + value[source_rows:]
        near_w[pl.ds(pl.multiple_of(k * source_rows, 8), source_rows), :] = value[:, :slots]
        near_c[pl.ds(pl.multiple_of(k * source_rows, 8), source_rows), :] = value[:, slots:]
        return 0

    def near_halo(k, _):
        far_x, far_y, far_z = 3 * (k // 4), 3 * (k // 2 % 2), 3 * (k % 2)
        columns = [(x, y) for x in (1, 2, far_x) for y in (1, 2, far_y)]
        total = None
        group = []
        for n, (x, y) in enumerate(columns):
            remote = n not in (0, 1, 3, 4)
            for z in (1, 2, far_z) if remote else (far_z,):
                group.append(
                    (halo_split[4 * x + y], target_rows[k, z], halo_rows[16 * x + 4 * y + z])
                )
            if n in (2, 5, 6, 7, 8):
                value = summed(group)
                total = value if total is None else total + value
                group = []
        total = total[:source_rows] + total[source_rows:]
        where = pl.ds(pl.multiple_of(k * source_rows, 8), source_rows)
        near_w[where, :] += total[:, :slots]
        near_c[where, :] += total[:, slots:]
        return 0

    lax.fori_loop(0, 4, near_local, 0)
    for copy in copies_z:
        copy.wait()
    copies_y = [line_copy(1, u, gathered.at[0], gathered.at[u]) for u in range(1, count_y)]
    for copy in copies_y:
        copy.start()

    sources = count_y * count_z * 8
    target = lax.broadcasted_iota(jnp.int32, (count_x * 8, sources), 0)
    source = lax.broadcasted_iota(jnp.int32, (count_x * 8, sources), 1)
    apart = [
        2 * (target // 8) + target // 4 % 2 - source // 4 % 2,
        2 * (source // (8 * count_z)) + target // 2 % 2 - source // 2 % 2,
        2 * (source // 8 % count_z) + target % 2 - source % 2,
    ]
    largest, total_sq = 0, 0
    for axis in range(3):
        extent = 2 * sizes[axis]
        steps = lax.rem(apart[axis] + extent, extent)
        steps = jnp.minimum(steps, extent - steps)
        largest = jnp.maximum(largest, steps)
        total_sq = total_sq + steps * steps
    weights = jnp.where(largest > 1, lax.rsqrt(jnp.maximum(total_sq, 1).astype(f32)), 0.0)
    weights_high, weights_low = two_parts(weights)
    weights = jnp.concatenate([weights_high, weights_low, weights_high], 1)

    translation = translation_ref[...]
    for m in range(3):
        value = translation if m == 0 else pltpu.roll(translation, slots - terms * m, 1)
        value = jnp.where(lax.broadcasted_iota(jnp.int32, (slots, slots), 1) < terms, value, 0.0)
        high, low = two_parts(value)
        translation_rows[:, pl.ds(2 * m * slots, slots)] = high
        translation_rows[:, pl.ds((2 * m + 1) * slots, slots)] = low

    lax.fori_loop(4, 8, near_local, 0)

    for copy in copies_y:
        copy.wait()
    high, low = two_parts(gathered[...].reshape(sources, slots))
    partial[...] = jnp.dot(
        weights, jnp.concatenate([high, high, low], 0), preferred_element_type=f32
    ).reshape(count_x, 8, slots)
    copies_x = [line_copy(0, u, partial.at[u], received.at[u]) for u in range(1, count_x)]
    for copy in copies_x:
        copy.start()

    for copy in copies_halo:
        copy.wait()

    def prepare(group, _):
        value = [eight_cells(halo, group, n) for n in range(9)]
        place = [
            jnp.zeros((8, slots), jnp.int32) + group // 2,
            group % 2 * 2 + cell // 4,
            cell % 4,
        ]
        position = [value[c] + (place[c].astype(f32) - 1.5) for c in range(3)]
        rows, splits = source_values(position, value[3:6], value[6:9])
        store_rows(stage_rows, rows, source_rows)
        store_rows(stage_split, splits, split_rows)
        pack_sources(
            stage_rows, stage_split, halo_rows, halo_split, group * 8, group * 2
        )
        return 0

    lax.fori_loop(0, 8, prepare, 0)
    lax.fori_loop(0, 8, near_halo, 0)

    def row(ref, n):
        return ref[pl.ds(n, 8, stride=source_rows), :]

    pairs = [charge[a] * lines[b] for a in range(3) for b in range(3)]
    still = sum(pairs[n] * row(near_w, n) for n in range(9))
    near = []
    for c in range(3):
        first = sum(pairs[n] * row(near_w, 9 + 9 * c + n) for n in range(9))
        second = row(near_c, 36 + c) - sum(position[b] * row(near_c, 3 * b + c) for b in range(3))
        near.append(near_scale * (first - position[c] * still + second))

    for copy in copies_x:
        copy.wait()
    summed_moments = partial[0]
    for u in range(1, count_x):
        summed_moments = summed_moments + received[u]
    high, low = high_low(summed_moments)
    product = jnp.dot(
        jnp.concatenate([high, low], 0).astype(bf16),
        translation_rows[...],
        preferred_element_type=f32,
    )
    product = product[:8] + product[8:]
    highs, lows = [], []
    for m in range(3):
        value = product[:, 2 * m * slots : (2 * m + 1) * slots]
        value = value + product[:, (2 * m + 1) * slots : (2 * m + 2) * slots]
        for part, result in zip(high_low(value), (highs, lows)):
            result.append(part + pltpu.roll(part, term_rows, 1))
    left = [jnp.concatenate(parts + [zero], 0).astype(bf16) for parts in (highs, lows)]
    right = jnp.concatenate([poly_rows[k] for k in range(8)], 1)
    fields = jnp.dot(
        jnp.concatenate(left, 1),
        jnp.concatenate([right, right], 0),
        preferred_element_type=f32,
    )
    far = []
    for m in range(3):
        value = zero
        for k in range(8):
            value = jnp.where(
                cell == k, fields[8 * m : 8 * m + 8, k * slots : (k + 1) * slots], value
            )
        far.append(value * mask)

    stressed = [sum(stress_ref[a, b] * charge[b] for b in range(3)) for a in range(3)]
    applied = crossed(stressed, lines)
    force = [near[c] + far[c] + applied[c] for c in range(3)]
    along = sum(force[c] * lines[c] for c in range(3))
    along = along / jnp.maximum(sum(lines[c] * lines[c] for c in range(3)), 1.0)
    scale = mobility * mask
    for c in range(3):
        out_ref[c] = scale * (force[c] - along * lines[c])


def body(sizes, offsets, lines, burgers, counts, mobility, stress, translation):
    vmem, smem = (pl.BlockSpec(memory_space=space) for space in (pltpu.VMEM, pltpu.SMEM))
    shape = offsets.shape
    flat = (3, 8, slots)
    longest = max(sizes)
    result = pl.pallas_call(
        functools.partial(kernel, sizes),
        out_shape=jax.ShapeDtypeStruct(flat, f32),
        in_specs=[vmem, vmem, vmem, smem, smem, smem, vmem],
        out_specs=vmem,
        scratch_shapes=[
            pltpu.VMEM((4, 4, 4, 16, slots), f32),
            pltpu.VMEM((sizes[1], sizes[2], 8, slots), f32),
            pltpu.VMEM((sizes[0], 8, slots), f32),
            pltpu.VMEM((sizes[0], 8, slots), f32),
            pltpu.VMEM((8 * source_rows, slots), f32),
            pltpu.VMEM((8 * split_rows, slots), f32),
            pltpu.VMEM((8 * term_rows, slots), f32),
            pltpu.VMEM((8, 2 * source_rows, slots), bf16),
            pltpu.VMEM((2, slots, 4 * split_rows), bf16),
            pltpu.VMEM((64, 2 * source_rows, slots), bf16),
            pltpu.VMEM((16, slots, 4 * split_rows), bf16),
            pltpu.VMEM((8, 4, 4 * split_rows, 2 * slots), bf16),
            pltpu.VMEM((8, slots, slots), bf16),
            pltpu.VMEM((slots, 6 * slots), bf16),
            pltpu.VMEM((8 * source_rows, slots), f32),
            pltpu.VMEM((8 * source_rows, slots), f32),
            pltpu.SemaphoreType.DMA((26,)),
            pltpu.SemaphoreType.DMA((26,)),
            pltpu.SemaphoreType.DMA((3, longest)),
            pltpu.SemaphoreType.DMA((3, longest)),
        ],
        compiler_params=pltpu.CompilerParams(
            collective_id=0, has_side_effects=True, vmem_limit_bytes=48 * 1024 * 1024
        ),
    )(
        offsets.reshape(flat),
        lines.reshape(flat),
        burgers.reshape(flat),
        counts,
        mobility,
        stress,
        translation,
    )
    return result.reshape(shape)


def solution(mesh):
    sizes = tuple(mesh.shape[name] for name in ("gx", "gy", "gz"))
    placed = (
        P(None, "gx", "gy", "gz", None),
        P(None, "gx", "gy", "gz", None),
        P(None, "gx", "gy", "gz", None),
        P("gx", "gy", "gz"),
        P("gx", "gy", "gz"),
        P(),
        P(),
    )
    return jax.shard_map(
        functools.partial(body, sizes),
        mesh=mesh,
        in_specs=placed,
        out_specs=P(None, "gx", "gy", "gz", None),
        check_vma=False,
    )
```

time: 187 us -> 44.3 us (0.24); the launches traced: 184 us -> 43.9 us
  other arithmetic: 96 us -> 0 us
  waiting for transfers between devices: 44.2 us -> 0 us
  Pallas kernels: 0 us -> 39 us
  starting transfers between devices: 22.7 us -> 0 us
  between operations: 13.7 us -> 0.02 us
  matrix products: 3.82 us -> 0 us
    reduce_sum x27 -> x0, other arithmetic: 59.8 us -> none  [the longest x26 59.5 us: pair_forces(): jnp.sum(first_coef * separation[column] + second_coef * source[3 + column...]
    all_gather x1 -> x0, waiting for transfers between devices: 44.2 us -> none  [body(): piece = lax.all_gather(moments, ('gx', 'gy', 'gz'), axis=0, tiled=True)]
    pallas_call x0 -> x1, Pallas kernels: none -> 39 us  [body(): pl.pallas_call(functools.partial(kernel, sizes), out_shape=jax.ShapeDtype...]
    ppermute x6 -> x0, starting transfers between devices: 22.7 us -> none  [the longest x3 16.7 us: padded_2(): after = lax.ppermute(first, axis, down)]
    unnamed x27 -> x0, other arithmetic: 19.2 us -> none
    sub x3 -> x0, other arithmetic: 7.11 us -> none  [the longest x1 4.47 us: crossed(): left[1] * right[2] - left[2] * right[1]]
    mul x16 -> x0, other arithmetic: 6.13 us -> none  [the longest x12 4.01 us: pair_forces(): target[3 + column][..., :, None] * source[3 + column][..., None, :]]
    dot_general x4 -> x0, matrix products: 3.82 us -> none  [the longest x1 3.03 us: body(): jnp.dot(weights, piece, precision=highest, preferred_element_type=jnp.flo...]
  transfers between devices with their start and end apart: 7 -> 0, of which waited for: 1 -> 0; matrix products, arithmetic and copies ran while one was open for 50% -> 0% of each run, Pallas kernels for 0% -> 0%
where the time goes in v1:
time: 44.3 us; the launch traced here: 43.9 us
  Pallas kernels  39 us (88%)
  local copies, waits for them, and re-layouts  4.94 us (11%)
    pallas_call x1, Pallas kernels, body(): pl.pallas_call(functools.partial(kernel, sizes), out_shape=jax.ShapeDtype...  39 us
    unnamed x15, local copies, waits for them, and re-layouts  4.94 us

profile of v1, /device:TPU:1, one launch (start us, length us, event | category | flops | bytes accessed | tf_op | source)
XLA Modules:
  0.0 43.9 jit_solution(11550393673991157393)
XLA Ops:
  0.0 0.0 copy-start.5
  0.0 0.0 copy-start.4
  0.0 0.7 %copy-done.5 = f32[2,2,2]{2,1,0:T(2,128)S(1)} copy-done((f32[2,2,2]{2,1,0:T(2,128)S(1)}, f32[2,2,2]{2,1,0:T(2,128)}, u32[]{:S(2)}) %copy-start.5) | copy-done | bytes 56
  0.7 0.0 copy-done.4
  0.7 0.0 copy-start
  0.7 0.8 %copy-done = f32[128,128]{1,0:T(8,128)S(1)} copy-done((f32[128,128]{1,0:T(8,128)S(1)}, f32[128,128]{1,0:T(8,128)}, u32[]{:S(2)}) %copy-start) | copy-done | bytes 65560
  1.5 0.0 copy-start.1
  1.5 0.7 %copy-done.1 = f32[3,2,2,2,128]{4,3,2,1,0:T(2,128)S(1)} copy-done((f32[3,2,2,2,128]{4,3,2,1,0:T(2,128)S(1)}, f32[3,2,2,2,128]{4,3,2,1,0:T(2,128)}, u32[]{:S(2)}) %copy-start.1) | copy-done | bytes 12312
  2.2 0.0 copy-start.2
  2.2 0.7 %copy-done.2 = f32[3,2,2,2,128]{4,3,2,1,0:T(2,128)S(1)} copy-done((f32[3,2,2,2,128]{4,3,2,1,0:T(2,128)S(1)}, f32[3,2,2,2,128]{4,3,2,1,0:T(2,128)}, u32[]{:S(2)}) %copy-start.2) | copy-done | bytes 12312
  3.0 0.0 copy-start.3
  3.0 0.7 %copy-done.3 = f32[3,2,2,2,128]{4,3,2,1,0:T(2,128)S(1)} copy-done((f32[3,2,2,2,128]{4,3,2,1,0:T(2,128)S(1)}, f32[3,2,2,2,128]{4,3,2,1,0:T(2,128)}, u32[]{:S(2)}) %copy-start.3) | copy-done | bytes 12312
  3.7 0.0 copy-start.6
  3.7 0.7 %copy-done.6 = f32[3,3]{1,0:T(4,128)S(1)} copy-done((f32[3,3]{1,0:T(4,128)S(1)}, f32[3,3]{1,0:T(4,128)}, u32[]{:S(2)}) %copy-start.6) | copy-done | bytes 60
  4.3 39.0 %shard_map.73 = f32[3,8,128]{2,1,0:T(8,128)S(1)} custom-call(f32[3,8,128]{2,1,0:T(8,128)S(1)} %bitcast.5, f32[3,8,128]{2,1,0:T(8,128)S(1)} %bitcast.6, f32[3,8,128]{2,1,0:T(8,128)S(1)} %bitcast.7, s32[2,2,2]{2,1,0:T(2,128)S(1)} %copy-done.4, f32[2,2,2]{2,1,0:T(2,128)S(1)} %copy-done.5, f32[3,3]{1,0:T(4,128)S(1)} %copy-done.6, f32[128,128]{1,0:T(8,128)S(1)} %copy-done), custom_call_target="tpu_custom_call" | custom-call | tf_op jit(solution)/shard_map/pallas_call | solution.py:470
  43.3 0.6 %copy.9 = f32[3,2,2,2,128]{4,3,2,1,0:T(2,128)} copy(f32[3,2,2,2,128]{4,3,2,1,0:T(2,128)S(1)} %bitcast.4) | data formatting | bytes 24576
Async XLA Ops:
  0.0 0.7 %copy-start.5 = (f32[2,2,2]{2,1,0:T(2,128)S(1)}, f32[2,2,2]{2,1,0:T(2,128)}, u32[]{:S(2)}) copy-start(f32[2,2,2]{2,1,0:T(2,128)} %mobility_ref.1) | copy-start | bytes 100
  0.0 0.7 %copy-start.4 = (s32[2,2,2]{2,1,0:T(2,128)S(1)}, s32[2,2,2]{2,1,0:T(2,128)}, u32[]{:S(2)}) copy-start(s32[2,2,2]{2,1,0:T(2,128)} %counts_ref.1) | copy-start | bytes 100
  0.7 0.8 %copy-start = (f32[128,128]{1,0:T(8,128)S(1)}, f32[128,128]{1,0:T(8,128)}, u32[]{:S(2)}) copy-start(f32[128,128]{1,0:T(8,128)} %translation_ref.1) | copy-start | bytes 196612
  1.5 0.7 %copy-start.1 = (f32[3,2,2,2,128]{4,3,2,1,0:T(2,128)S(1)}, f32[3,2,2,2,128]{4,3,2,1,0:T(2,128)}, u32[]{:S(2)}) copy-start(f32[3,2,2,2,128]{4,3,2,1,0:T(2,128)} %param.7) | copy-start | bytes 36868
  2.2 0.7 %copy-start.2 = (f32[3,2,2,2,128]{4,3,2,1,0:T(2,128)S(1)}, f32[3,2,2,2,128]{4,3,2,1,0:T(2,128)}, u32[]{:S(2)}) copy-start(f32[3,2,2,2,128]{4,3,2,1,0:T(2,128)} %param.8) | copy-start | bytes 36868
  3.0 0.7 %copy-start.3 = (f32[3,2,2,2,128]{4,3,2,1,0:T(2,128)S(1)}, f32[3,2,2,2,128]{4,3,2,1,0:T(2,128)}, u32[]{:S(2)}) copy-start(f32[3,2,2,2,128]{4,3,2,1,0:T(2,128)} %param.9) | copy-start | bytes 36868
  3.7 0.7 %copy-start.6 = (f32[3,3]{1,0:T(4,128)S(1)}, f32[3,3]{1,0:T(4,128)}, u32[]{:S(2)}) copy-start(f32[3,3]{1,0:T(4,128)} %stress_ref.1) | copy-start | bytes 112

commit v2 on v1

--- a/solution.py
+++ b/solution.py
@@ -105,35 +105,93 @@
 
 
 def pack_sources(stage_rows, stage_split, out_rows, out_split, first, first_split):
+    zero = jnp.zeros((source_rows, slots), f32)
     for cell in range(8):
         value = stage_rows[pl.ds(cell * source_rows, source_rows), :]
         high, low = high_low(value)
-        out_rows[first + cell] = jnp.concatenate([high, low], 0).astype(bf16)
+        out_rows[first + cell, :, pl.ds(0, slots)] = jnp.concatenate([high, low], 0).astype(bf16)
+        out_rows[first + cell, :, pl.ds(slots, slots)] = jnp.concatenate([high, zero], 0).astype(
+            bf16
+        )
     for half in range(2):
         value = stage_split[pl.ds(half * 4 * split_rows, 4 * split_rows), :]
         out_split[first_split + half] = value.T.astype(bf16)
 
 
-def pair_weights(split, target):
-    both = jnp.dot(split, target, preferred_element_type=f32)
-    inverse = lax.rsqrt(both[:, :slots])
-    square = inverse * inverse
-    cube = square * inverse
-    value = jnp.concatenate([cube, cube * square * both[:, slots:]], 1)
-    return two_parts(value)
-
-
-def summed(items):
-    highs, lows, rows = [], [], []
-    for split, target, row in items:
-        high, low = pair_weights(split, target)
-        highs.append(high)
-        lows.append(low)
-        rows.append(row)
-    return jnp.dot(
-        jnp.concatenate(rows + rows, 1),
-        jnp.concatenate(highs + lows, 0),
-        preferred_element_type=f32,
+def product(pairs, unit=0, transpose=False):
+    def scope(total):
+        for n, (left, right) in enumerate(pairs):
+            pltpu.matmul_push_rhs(right, n % 2, unit, transpose=transpose)
+            pltpu.matmul_acc_lhs(total, left, load_staged_rhs=n % 2)
+        return pltpu.matmul_pop(total)
+
+    return pl.run_scoped(scope, pltpu.ACC(unit)((pairs[0][0].shape[0], 2 * slots), f32))
+
+
+chunk = 32
+chunks = slots // chunk
+ahead = 4
+
+
+def near_sums(blocks, plan, target_rows, store):
+    count = len(blocks)
+    held = next(n for n in range(ahead, 2 * ahead) if (count - ahead) % n == 0)
+
+    def scope(total, *buffers):
+        def buffer(p, n):
+            return buffers[p % held * chunks + n]
+
+        def start(p, k):
+            first = p == 0 or blocks[p] != blocks[p - 1]
+            block, splits, index, _, _ = plan(k, p)
+            if first:
+                rhs = target_rows[k, block]
+                rhs = jnp.concatenate([rhs, jnp.zeros((slots, 2 * slots), bf16)], 0)
+                pltpu.matmul_push_rhs(rhs, 0, 0)
+            for n in range(chunks):
+                left = splits[index, pl.ds(n * chunk, chunk), :]
+                left = jnp.concatenate([left, jnp.zeros((chunk, slots), bf16)], 1)
+                load = 0 if first and n == 0 else None
+                pltpu.matmul_acc_lhs(buffer(p, n), left, load_staged_rhs=load)
+
+        def finish(p, k):
+            highs, lows = [], []
+            for n in range(chunks):
+                both = pltpu.matmul_pop(buffer(p, n))
+                inverse = lax.rsqrt(both[:, :slots])
+                square = inverse * inverse
+                cube = square * inverse
+                value = jnp.concatenate([cube, cube * square * both[:, slots:]], 1)
+                high, low = two_parts(value)
+                highs.append(high)
+                lows.append(low)
+            if p == 0:
+                store(jnp.maximum(k - 1, 0), pltpu.matmul_pop(total))
+            _, _, _, rows, place = plan(k, p)
+            pltpu.matmul_push_rhs(jnp.concatenate(highs + lows, 0), p % 2, 1)
+            pltpu.matmul_acc_lhs(total, rows[place], load_staged_rhs=p % 2)
+
+        def target(k, _):
+            for p in range(count):
+                finish(p, k)
+                if p + ahead < count:
+                    start(p + ahead, k)
+                else:
+                    start(p + ahead - count, jnp.minimum(k + 1, 7))
+            return 0
+
+        for p in range(ahead):
+            start(p, 0)
+        lax.fori_loop(0, 8, target, 0)
+        store(7, pltpu.matmul_pop(total))
+        for p in range(ahead):
+            for n in range(chunks):
+                pltpu.matmul_pop(buffer(p, n))
+
+    pl.run_scoped(
+        scope,
+        pltpu.ACC(1)((2 * source_rows, 2 * slots), f32),
+        *[pltpu.ACC(0)((chunk, 2 * slots), f32)] * (held * chunks),
     )
 
 
@@ -163,6 +221,8 @@
     translation_rows,
     near_w,
     near_c,
+    halo_w,
+    halo_c,
     halo_send,
     halo_recv,
     line_send,
@@ -222,18 +282,18 @@
         highs.append(high)
         lows.append(low)
     zero = jnp.zeros((8, slots), f32)
-    left = []
-    for parts in (highs, lows):
-        for k in range(8):
-            rows = [jnp.where(cell == k, part, 0.0) for part in parts] + [zero]
+    pairs = []
+    for first in range(0, 8, 2):
+        left = []
+        for k in (first, first + 1):
+            rows = [jnp.where(cell == k, part, 0.0) for part in highs] + [zero]
+            rows += [jnp.where(cell == k, part, 0.0) for part in lows] + [zero]
             left.append(jnp.concatenate(rows, 0).astype(bf16))
-    right = [poly_rows[k] for k in range(8)]
-    moments = lax.dot_general(
-        jnp.concatenate(left, 1),
-        jnp.concatenate(right + right, 1),
-        (((1,), (1,)), ((), ())),
-        preferred_element_type=f32,
-    )
+        right = jnp.concatenate([poly_rows[first], poly_rows[first + 1]], 1)
+        right = jnp.concatenate([right, jnp.zeros((slots, 2 * slots), bf16)], 0)
+        pairs.append((jnp.concatenate(left, 1), right))
+    moments = product(pairs, transpose=True)[:, :slots]
+    moments = moments[:32] + moments[32:]
     total = zero
     for m in range(3):
         part = moments[8 * m : 8 * m + 8]
@@ -306,40 +366,36 @@
                     k, block, pl.ds(block * split_rows, split_rows), pl.ds(side * slots, slots)
                 ] = value
 
-    def near_local(k, _):
-        items = []
-        for source in range(8):
-            items.append(
-                (local_split[source // 4], target_rows[k, source % 4], local_rows[source])
-            )
-        value = summed(items)
+    local_order = [4 * half + place for place in range(4) for half in range(2)]
+
+    def local_plan(k, p):
+        source = local_order[p]
+        return source % 4, local_split, source // 4, local_rows, source
+
+    def keep(ref_w, ref_c, k, value):
         value = value[:source_rows] + value[source_rows:]
-        near_w[pl.ds(pl.multiple_of(k * source_rows, 8), source_rows), :] = value[:, :slots]
-        near_c[pl.ds(pl.multiple_of(k * source_rows, 8), source_rows), :] = value[:, slots:]
-        return 0
-
-    def near_halo(k, _):
-        far_x, far_y, far_z = 3 * (k // 4), 3 * (k // 2 % 2), 3 * (k % 2)
-        columns = [(x, y) for x in (1, 2, far_x) for y in (1, 2, far_y)]
-        total = None
-        group = []
-        for n, (x, y) in enumerate(columns):
-            remote = n not in (0, 1, 3, 4)
-            for z in (1, 2, far_z) if remote else (far_z,):
-                group.append(
-                    (halo_split[4 * x + y], target_rows[k, z], halo_rows[16 * x + 4 * y + z])
-                )
-            if n in (2, 5, 6, 7, 8):
-                value = summed(group)
-                total = value if total is None else total + value
-                group = []
-        total = total[:source_rows] + total[source_rows:]
         where = pl.ds(pl.multiple_of(k * source_rows, 8), source_rows)
-        near_w[where, :] += total[:, :slots]
-        near_c[where, :] += total[:, slots:]
-        return 0
-
-    lax.fori_loop(0, 4, near_local, 0)
+        ref_w[where, :] = value[:, :slots]
+        ref_c[where, :] = value[:, slots:]
+
+    halo_order = [(n, z) for z in range(3) for n in range(9) if z == 2 or n in (2, 5, 6, 7, 8)]
+
+    def halo_plan(k, p):
+        n, z = halo_order[p]
+        x = (1, 2, 3 * (k // 4))[n // 3]
+        y = (1, 2, 3 * (k // 2 % 2))[n % 3]
+        z = (1, 2, 3 * (k % 2))[z]
+        return z, halo_split, 4 * x + y, halo_rows, 16 * x + 4 * y + z
+
+    def near_local():
+        blocks = [source % 4 for source in local_order]
+        near_sums(blocks, local_plan, target_rows, functools.partial(keep, near_w, near_c))
+
+    def near_halo():
+        blocks = [z for _, z in halo_order]
+        near_sums(blocks, halo_plan, target_rows, functools.partial(keep, halo_w, halo_c))
+
+    near_local()
     for copy in copies_z:
         copy.wait()
     copies_y = [line_copy(1, u, gathered.at[0], gathered.at[u]) for u in range(1, count_y)]
@@ -362,8 +418,7 @@
         largest = jnp.maximum(largest, steps)
         total_sq = total_sq + steps * steps
     weights = jnp.where(largest > 1, lax.rsqrt(jnp.maximum(total_sq, 1).astype(f32)), 0.0)
-    weights_high, weights_low = two_parts(weights)
-    weights = jnp.concatenate([weights_high, weights_low, weights_high], 1)
+    weights = jnp.concatenate(two_parts(weights), 0)
 
     translation = translation_ref[...]
     for m in range(3):
@@ -373,14 +428,16 @@
         translation_rows[:, pl.ds(2 * m * slots, slots)] = high
         translation_rows[:, pl.ds((2 * m + 1) * slots, slots)] = low
 
-    lax.fori_loop(4, 8, near_local, 0)
 
     for copy in copies_y:
         copy.wait()
-    high, low = two_parts(gathered[...].reshape(sources, slots))
-    partial[...] = jnp.dot(
-        weights, jnp.concatenate([high, high, low], 0), preferred_element_type=f32
-    ).reshape(count_x, 8, slots)
+    right = jnp.concatenate(two_parts(gathered[...].reshape(sources, slots)), 1)
+    value = product(
+        [(weights[:, n : n + 256], right[n : n + 256]) for n in range(0, sources, 256)]
+    )
+    value = value[: 8 * count_x] + value[8 * count_x :]
+    value = value[:, :slots] + value[:, slots:]
+    partial[...] = value.reshape(count_x, 8, slots)
     copies_x = [line_copy(0, u, partial.at[u], received.at[u]) for u in range(1, count_x)]
     for copy in copies_x:
         copy.start()
@@ -405,10 +462,12 @@
         return 0
 
     lax.fori_loop(0, 8, prepare, 0)
-    lax.fori_loop(0, 8, near_halo, 0)
-
-    def row(ref, n):
-        return ref[pl.ds(n, 8, stride=source_rows), :]
+    near_halo()
+
+    def row(refs, n):
+        return sum(ref[pl.ds(n, 8, stride=source_rows), :] for ref in refs)
+
+    near_w, near_c = (near_w, halo_w), (near_c, halo_c)
 
     pairs = [charge[a] * lines[b] for a in range(3) for b in range(3)]
     still = sum(pairs[n] * row(near_w, n) for n in range(9))
@@ -424,33 +483,28 @@
     for u in range(1, count_x):
         summed_moments = summed_moments + received[u]
     high, low = high_low(summed_moments)
-    product = jnp.dot(
-        jnp.concatenate([high, low], 0).astype(bf16),
-        translation_rows[...],
-        preferred_element_type=f32,
-    )
-    product = product[:8] + product[8:]
+    left = jnp.concatenate([high, low], 0).astype(bf16)
+    left = jnp.concatenate([left, jnp.zeros((16, slots), bf16)], 1)
     highs, lows = [], []
     for m in range(3):
-        value = product[:, 2 * m * slots : (2 * m + 1) * slots]
-        value = value + product[:, (2 * m + 1) * slots : (2 * m + 2) * slots]
+        right = translation_rows[:, pl.ds(2 * m * slots, 2 * slots)]
+        right = jnp.concatenate([right, jnp.zeros((slots, 2 * slots), bf16)], 0)
+        value = product([(left, right)], m % 2)
+        value = value[:8] + value[8:]
+        value = value[:, :slots] + value[:, slots:]
         for part, result in zip(high_low(value), (highs, lows)):
             result.append(part + pltpu.roll(part, term_rows, 1))
     left = [jnp.concatenate(parts + [zero], 0).astype(bf16) for parts in (highs, lows)]
-    right = jnp.concatenate([poly_rows[k] for k in range(8)], 1)
-    fields = jnp.dot(
-        jnp.concatenate(left, 1),
-        jnp.concatenate([right, right], 0),
-        preferred_element_type=f32,
-    )
-    far = []
-    for m in range(3):
-        value = zero
-        for k in range(8):
-            value = jnp.where(
-                cell == k, fields[8 * m : 8 * m + 8, k * slots : (k + 1) * slots], value
-            )
-        far.append(value * mask)
+    left = jnp.concatenate(left, 1)
+    far = [zero] * 3
+    for first in range(0, 8, 2):
+        right = jnp.concatenate([poly_rows[first], poly_rows[first + 1]], 1)
+        fields = product([(left, jnp.concatenate([right, right], 0))], first // 2 % 2)
+        for m in range(3):
+            for n in range(2):
+                field = fields[8 * m : 8 * m + 8, n * slots : (n + 1) * slots]
+                far[m] = jnp.where(cell == first + n, field, far[m])
+    far = [value * mask for value in far]
 
     stressed = [sum(stress_ref[a, b] * charge[b] for b in range(3)) for a in range(3)]
     applied = crossed(stressed, lines)
@@ -480,13 +534,15 @@
             pltpu.VMEM((8 * source_rows, slots), f32),
             pltpu.VMEM((8 * split_rows, slots), f32),
             pltpu.VMEM((8 * term_rows, slots), f32),
-            pltpu.VMEM((8, 2 * source_rows, slots), bf16),
+            pltpu.VMEM((8, 2 * source_rows, 2 * slots), bf16),
             pltpu.VMEM((2, slots, 4 * split_rows), bf16),
-            pltpu.VMEM((64, 2 * source_rows, slots), bf16),
+            pltpu.VMEM((64, 2 * source_rows, 2 * slots), bf16),
             pltpu.VMEM((16, slots, 4 * split_rows), bf16),
             pltpu.VMEM((8, 4, 4 * split_rows, 2 * slots), bf16),
             pltpu.VMEM((8, slots, slots), bf16),
             pltpu.VMEM((slots, 6 * slots), bf16),
+            pltpu.VMEM((8 * source_rows, slots), f32),
+            pltpu.VMEM((8 * source_rows, slots), f32),
             pltpu.VMEM((8 * source_rows, slots), f32),
             pltpu.VMEM((8 * source_rows, slots), f32),
             pltpu.SemaphoreType.DMA((26,)),

time: 44.3 us -> 41.6 us (0.939)
  Pallas kernels: 39 us -> 36.2 us
    pallas_call x1, Pallas kernels: 39 us -> 36.2 us  [body(): pl.pallas_call(functools.partial(kernel, sizes), out_shape=jax.ShapeDtype...]
where the time goes in v2:
time: 41.6 us; the launch traced here: 41.2 us
  Pallas kernels  36.2 us (87%)
  local copies, waits for them, and re-layouts  4.94 us (12%)
    pallas_call x1, Pallas kernels, body(): pl.pallas_call(functools.partial(kernel, sizes), out_shape=jax.ShapeDtype...  36.2 us
    unnamed x15, local copies, waits for them, and re-layouts  4.94 us

profile of v2, /device:TPU:1, one launch (start us, length us, event | category | flops | bytes accessed | tf_op | source)
XLA Modules:
  0.0 41.2 jit_solution(9630921565628752848)
XLA Ops:
  0.0 0.0 copy-start.5
  0.0 0.0 copy-start.4
  0.0 0.7 %copy-done.5 = f32[2,2,2]{2,1,0:T(2,128)S(1)} copy-done((f32[2,2,2]{2,1,0:T(2,128)S(1)}, f32[2,2,2]{2,1,0:T(2,128)}, u32[]{:S(2)}) %copy-start.5) | copy-done | bytes 56
  0.7 0.0 copy-done.4
  0.7 0.0 copy-start
  0.7 0.8 %copy-done = f32[128,128]{1,0:T(8,128)S(1)} copy-done((f32[128,128]{1,0:T(8,128)S(1)}, f32[128,128]{1,0:T(8,128)}, u32[]{:S(2)}) %copy-start) | copy-done | bytes 65560
  1.5 0.0 copy-start.1
  1.5 0.7 %copy-done.1 = f32[3,2,2,2,128]{4,3,2,1,0:T(2,128)S(1)} copy-done((f32[3,2,2,2,128]{4,3,2,1,0:T(2,128)S(1)}, f32[3,2,2,2,128]{4,3,2,1,0:T(2,128)}, u32[]{:S(2)}) %copy-start.1) | copy-done | bytes 12312
  2.2 0.0 copy-start.2
  2.2 0.7 %copy-done.2 = f32[3,2,2,2,128]{4,3,2,1,0:T(2,128)S(1)} copy-done((f32[3,2,2,2,128]{4,3,2,1,0:T(2,128)S(1)}, f32[3,2,2,2,128]{4,3,2,1,0:T(2,128)}, u32[]{:S(2)}) %copy-start.2) | copy-done | bytes 12312
  3.0 0.0 copy-start.3
  3.0 0.7 %copy-done.3 = f32[3,2,2,2,128]{4,3,2,1,0:T(2,128)S(1)} copy-done((f32[3,2,2,2,128]{4,3,2,1,0:T(2,128)S(1)}, f32[3,2,2,2,128]{4,3,2,1,0:T(2,128)}, u32[]{:S(2)}) %copy-start.3) | copy-done | bytes 12312
  3.7 0.0 copy-start.6
  3.7 0.7 %copy-done.6 = f32[3,3]{1,0:T(4,128)S(1)} copy-done((f32[3,3]{1,0:T(4,128)S(1)}, f32[3,3]{1,0:T(4,128)}, u32[]{:S(2)}) %copy-start.6) | copy-done | bytes 60
  4.3 36.2 %shard_map.73 = f32[3,8,128]{2,1,0:T(8,128)S(1)} custom-call(f32[3,8,128]{2,1,0:T(8,128)S(1)} %bitcast.5, f32[3,8,128]{2,1,0:T(8,128)S(1)} %bitcast.6, f32[3,8,128]{2,1,0:T(8,128)S(1)} %bitcast.7, s32[2,2,2]{2,1,0:T(2,128)S(1)} %copy-done.4, f32[2,2,2]{2,1,0:T(2,128)S(1)} %copy-done.5, f32[3,3]{1,0:T(4,128)S(1)} %copy-done.6, f32[128,128]{1,0:T(8,128)S(1)} %copy-done), custom_call_target="tpu_custom_call" | custom-call | tf_op jit(solution)/shard_map/pallas_call | solution.py:524
  40.6 0.6 %copy.9 = f32[3,2,2,2,128]{4,3,2,1,0:T(2,128)} copy(f32[3,2,2,2,128]{4,3,2,1,0:T(2,128)S(1)} %bitcast.4) | data formatting | bytes 24576
Async XLA Ops:
  0.0 0.7 %copy-start.5 = (f32[2,2,2]{2,1,0:T(2,128)S(1)}, f32[2,2,2]{2,1,0:T(2,128)}, u32[]{:S(2)}) copy-start(f32[2,2,2]{2,1,0:T(2,128)} %mobility_ref.1) | copy-start | bytes 100
  0.0 0.7 %copy-start.4 = (s32[2,2,2]{2,1,0:T(2,128)S(1)}, s32[2,2,2]{2,1,0:T(2,128)}, u32[]{:S(2)}) copy-start(s32[2,2,2]{2,1,0:T(2,128)} %counts_ref.1) | copy-start | bytes 100
  0.7 0.8 %copy-start = (f32[128,128]{1,0:T(8,128)S(1)}, f32[128,128]{1,0:T(8,128)}, u32[]{:S(2)}) copy-start(f32[128,128]{1,0:T(8,128)} %translation_ref.1) | copy-start | bytes 196612
  1.5 0.7 %copy-start.1 = (f32[3,2,2,2,128]{4,3,2,1,0:T(2,128)S(1)}, f32[3,2,2,2,128]{4,3,2,1,0:T(2,128)}, u32[]{:S(2)}) copy-start(f32[3,2,2,2,128]{4,3,2,1,0:T(2,128)} %param.7) | copy-start | bytes 36868
  2.2 0.7 %copy-start.2 = (f32[3,2,2,2,128]{4,3,2,1,0:T(2,128)S(1)}, f32[3,2,2,2,128]{4,3,2,1,0:T(2,128)}, u32[]{:S(2)}) copy-start(f32[3,2,2,2,128]{4,3,2,1,0:T(2,128)} %param.8) | copy-start | bytes 36868
  3.0 0.7 %copy-start.3 = (f32[3,2,2,2,128]{4,3,2,1,0:T(2,128)S(1)}, f32[3,2,2,2,128]{4,3,2,1,0:T(2,128)}, u32[]{:S(2)}) copy-start(f32[3,2,2,2,128]{4,3,2,1,0:T(2,128)} %param.9) | copy-start | bytes 36868
  3.7 0.7 %copy-start.6 = (f32[3,3]{1,0:T(4,128)S(1)}, f32[3,3]{1,0:T(4,128)}, u32[]{:S(2)}) copy-start(f32[3,3]{1,0:T(4,128)} %stress_ref.1) | copy-start | bytes 112

commit v3 on v2

--- a/solution.py
+++ b/solution.py
@@ -118,14 +118,21 @@
         out_split[first_split + half] = value.T.astype(bf16)
 
 
-def product(pairs, unit=0, transpose=False):
-    def scope(total):
-        for n, (left, right) in enumerate(pairs):
-            pltpu.matmul_push_rhs(right, n % 2, unit, transpose=transpose)
-            pltpu.matmul_acc_lhs(total, left, load_staged_rhs=n % 2)
-        return pltpu.matmul_pop(total)
-
-    return pl.run_scoped(scope, pltpu.ACC(unit)((pairs[0][0].shape[0], 2 * slots), f32))
+def products(groups, transpose=False):
+    def scope(*totals):
+        turn = [0, 0]
+        for n, pairs in enumerate(groups):
+            for left, right in pairs:
+                staged = turn[n % 2] % 2
+                turn[n % 2] += 1
+                pltpu.matmul_push_rhs(right, staged, n % 2, transpose=transpose)
+                pltpu.matmul_acc_lhs(totals[n], left, load_staged_rhs=staged)
+        return [pltpu.matmul_pop(total) for total in totals]
+
+    accumulators = [
+        pltpu.ACC(n % 2)((pairs[0][0].shape[0], 2 * slots), f32) for n, pairs in enumerate(groups)
+    ]
+    return pl.run_scoped(scope, *accumulators)
 
 
 chunk = 32
@@ -141,18 +148,26 @@
         def buffer(p, n):
             return buffers[p % held * chunks + n]
 
-        def start(p, k):
-            first = p == 0 or blocks[p] != blocks[p - 1]
-            block, splits, index, _, _ = plan(k, p)
-            if first:
-                rhs = target_rows[k, block]
-                rhs = jnp.concatenate([rhs, jnp.zeros((slots, 2 * slots), bf16)], 0)
-                pltpu.matmul_push_rhs(rhs, 0, 0)
+        def stage(p, k):
+            block = plan(k, p)[0]
+            rhs = jnp.concatenate([target_rows[k, block], jnp.zeros((slots, 2 * slots), bf16)], 0)
+            pltpu.matmul_push_rhs(rhs, 0, 0)
+
+        firsts = [p for p in range(count) if p == 0 or blocks[p] != blocks[p - 1]]
+
+        def start(p, k, after):
+            _, splits, index, _, _ = plan(k, p)
             for n in range(chunks):
                 left = splits[index, pl.ds(n * chunk, chunk), :]
                 left = jnp.concatenate([left, jnp.zeros((chunk, slots), bf16)], 1)
-                load = 0 if first and n == 0 else None
+                load = 0 if p in firsts and n == 0 else None
                 pltpu.matmul_acc_lhs(buffer(p, n), left, load_staged_rhs=load)
+            if p in firsts:
+                later = firsts.index(p) + 1
+                if later < len(firsts):
+                    stage(firsts[later], k)
+                else:
+                    stage(0, after)
 
         def finish(p, k):
             highs, lows = [], []
@@ -172,18 +187,23 @@
             pltpu.matmul_acc_lhs(total, rows[place], load_staged_rhs=p % 2)
 
         def target(k, _):
+            after = jnp.minimum(k + 1, 7)
             for p in range(count):
                 finish(p, k)
                 if p + ahead < count:
-                    start(p + ahead, k)
+                    start(p + ahead, k, after)
                 else:
-                    start(p + ahead - count, jnp.minimum(k + 1, 7))
+                    start(p + ahead - count, after, after)
             return 0
 
+        stage(0, 0)
         for p in range(ahead):
-            start(p, 0)
+            start(p, 0, 1)
         lax.fori_loop(0, 8, target, 0)
         store(7, pltpu.matmul_pop(total))
+        pltpu.matmul_acc_lhs(
+            buffer(0, 0), jnp.zeros((chunk, 2 * slots), bf16), load_staged_rhs=0
+        )
         for p in range(ahead):
             for n in range(chunks):
                 pltpu.matmul_pop(buffer(p, n))
@@ -197,6 +217,14 @@
 
 def kernel(
     sizes,
+    offsets_in,
+    lines_in,
+    burgers_in,
+    counts_in,
+    mobility_in,
+    stress_in,
+    translation_in,
+    out_ref,
     offsets_ref,
     lines_ref,
     burgers_ref,
@@ -204,7 +232,7 @@
     mobility_ref,
     stress_ref,
     translation_ref,
-    out_ref,
+    operand_sem,
     halo,
     gathered,
     partial,
@@ -219,15 +247,34 @@
     target_rows,
     poly_rows,
     translation_rows,
+    weight_rows,
     near_w,
     near_c,
     halo_w,
     halo_c,
     halo_send,
     halo_recv,
-    line_send,
-    line_recv,
+    gather_send,
+    gather_recv,
+    reduce_send,
+    reduce_recv,
 ):
+    operands = [
+        (counts_in, counts_ref),
+        (offsets_in, offsets_ref),
+        (lines_in, lines_ref),
+        (burgers_in, burgers_ref),
+        (mobility_in, mobility_ref),
+        (stress_in, stress_ref),
+        (translation_in, translation_ref),
+    ]
+    loads = [
+        pltpu.make_async_copy(source, target, operand_sem.at[n])
+        for n, (source, target) in enumerate(operands)
+    ]
+    for load in loads:
+        load.start()
+
     me = [lax.axis_index(name) for name in ("gx", "gy", "gz")]
     count_x, count_y, count_z = sizes
 
@@ -237,22 +284,46 @@
             for axis, step in enumerate((step_x, step_y, step_z))
         )
 
+    chips = count_y // 2
+    core = lax.rem(me[1], 2)
+    over = 1 - 2 * core
+    sources = [(r, b) for r in range(2) for b in range(count_z) if (r, b) != (0, 0)]
+    goals = [(u, v) for u in range(count_x) for v in range(chips) if (u, v) != (0, 0)]
     partners = list(offsets_26)
-    partners += [(u, 0, 0) for u in range(1, count_x) if u not in (1, count_x - 1)]
-    partners += [(0, u, 0) for u in range(1, count_y) if u not in (1, count_y - 1)]
-    partners += [(0, 0, u) for u in range(1, count_z) if u not in (1, count_z - 1)]
+    partners += [(0, r * over, b) for r, b in sources if b not in (0, 1, count_z - 1)]
+    partners += [(u, 2 * v, 0) for u, v in goals if v or u not in (1, count_x - 1)]
     barrier = pltpu.get_barrier_semaphore()
     for step in partners:
         pl.semaphore_signal(barrier, inc=1, device_id=device(*step), device_id_type=MESH)
 
+    shape = (count_x * chips * 8, 2 * count_z * 8)
+    goal = lax.broadcasted_iota(jnp.int32, shape, 0)
+    source = lax.broadcasted_iota(jnp.int32, shape, 1)
+    apart = [
+        2 * (goal // (8 * chips)) + goal // 4 % 2 - source // 4 % 2,
+        4 * (goal // 8 % chips) - 2 * over * (source // (8 * count_z)) + goal // 2 % 2 - source // 2 % 2,
+        2 * (source // 8 % count_z) + goal % 2 - source % 2,
+    ]
+    largest, total_sq = 0, 0
+    for axis in range(3):
+        extent = 2 * sizes[axis]
+        steps = lax.rem(apart[axis] + extent, extent)
+        steps = jnp.minimum(steps, extent - steps)
+        largest = jnp.maximum(largest, steps)
+        total_sq = total_sq + steps * steps
+    weights = jnp.where(largest > 1, lax.rsqrt(jnp.maximum(total_sq, 1).astype(f32)), 0.0)
+    weight_rows[...] = jnp.concatenate(two_parts(weights), 1)
+
+    target_rows[...] = jnp.zeros(target_rows.shape, bf16)
+
+    for load in loads[:4]:
+        load.wait()
     cell = lax.broadcasted_iota(jnp.int32, (8, slots), 0)
     lane = lax.broadcasted_iota(jnp.int32, (8, slots), 1)
     counts = jnp.zeros((8, slots), jnp.int32)
-    mobility = jnp.zeros((8, slots), f32)
     for k in range(8):
         where = (k // 4, k // 2 % 2, k % 2)
         counts = jnp.where(cell == k, counts_ref[where], counts)
-        mobility = jnp.where(cell == k, mobility_ref[where], mobility)
     mask = jnp.where(lane < counts, 1.0, 0.0).astype(f32)
     offsets = [offsets_ref[c] for c in range(3)]
     lines = [lines_ref[c] for c in range(3)]
@@ -292,7 +363,7 @@
         right = jnp.concatenate([poly_rows[first], poly_rows[first + 1]], 1)
         right = jnp.concatenate([right, jnp.zeros((slots, 2 * slots), bf16)], 0)
         pairs.append((jnp.concatenate(left, 1), right))
-    moments = product(pairs, transpose=True)[:, :slots]
+    moments = sum(products([pairs[:2], pairs[2:]], transpose=True))[:, :slots]
     moments = moments[:32] + moments[32:]
     total = zero
     for m in range(3):
@@ -310,22 +381,18 @@
 
     pl.semaphore_wait(barrier, len(partners))
 
-    def line_copy(axis, u, source, target):
-        step = [0, 0, 0]
-        step[axis] = u
-        return pltpu.make_async_remote_copy(
-            src_ref=source,
-            dst_ref=target,
-            send_sem=line_send.at[axis, u],
-            recv_sem=line_recv.at[axis, u],
-            device_id=device(*step),
+    copies_in = [
+        pltpu.make_async_remote_copy(
+            src_ref=gathered.at[0, 0],
+            dst_ref=gathered.at[r, b],
+            send_sem=gather_send.at[r, b],
+            recv_sem=gather_recv.at[r, b],
+            device_id=device(0, r * over, b),
             device_id_type=MESH,
         )
-
-    copies_z = [
-        line_copy(2, u, gathered.at[0, 0], gathered.at[0, u]) for u in range(1, count_z)
+        for r, b in sources
     ]
-    for copy in copies_z:
+    for copy in copies_in:
         copy.start()
     sides = {
         -1: (pl.ds(1, 1), pl.ds(3, 1)),
@@ -356,7 +423,6 @@
     store_rows(stage_split, splits, split_rows)
     pack_sources(stage_rows, stage_split, local_rows, local_split, 0, 0)
     distance, along = target_values(position, charge)
-    target_rows[...] = jnp.zeros(target_rows.shape, bf16)
     for side, values in enumerate((distance, along)):
         store_rows(stage_split, values, split_rows)
         for k in range(8):
@@ -396,30 +462,12 @@
         near_sums(blocks, halo_plan, target_rows, functools.partial(keep, halo_w, halo_c))
 
     near_local()
-    for copy in copies_z:
-        copy.wait()
-    copies_y = [line_copy(1, u, gathered.at[0], gathered.at[u]) for u in range(1, count_y)]
-    for copy in copies_y:
-        copy.start()
-
-    sources = count_y * count_z * 8
-    target = lax.broadcasted_iota(jnp.int32, (count_x * 8, sources), 0)
-    source = lax.broadcasted_iota(jnp.int32, (count_x * 8, sources), 1)
-    apart = [
-        2 * (target // 8) + target // 4 % 2 - source // 4 % 2,
-        2 * (source // (8 * count_z)) + target // 2 % 2 - source // 2 % 2,
-        2 * (source // 8 % count_z) + target % 2 - source % 2,
-    ]
-    largest, total_sq = 0, 0
-    for axis in range(3):
-        extent = 2 * sizes[axis]
-        steps = lax.rem(apart[axis] + extent, extent)
-        steps = jnp.minimum(steps, extent - steps)
-        largest = jnp.maximum(largest, steps)
-        total_sq = total_sq + steps * steps
-    weights = jnp.where(largest > 1, lax.rsqrt(jnp.maximum(total_sq, 1).astype(f32)), 0.0)
-    weights = jnp.concatenate(two_parts(weights), 0)
-
+    for load in loads[4:]:
+        load.wait()
+    mobility = jnp.zeros((8, slots), f32)
+    for k in range(8):
+        where = (k // 4, k // 2 % 2, k % 2)
+        mobility = jnp.where(cell == k, mobility_ref[where], mobility)
     translation = translation_ref[...]
     for m in range(3):
         value = translation if m == 0 else pltpu.roll(translation, slots - terms * m, 1)
@@ -429,17 +477,28 @@
         translation_rows[:, pl.ds((2 * m + 1) * slots, slots)] = low
 
 
-    for copy in copies_y:
+    for copy in copies_in:
         copy.wait()
-    right = jnp.concatenate(two_parts(gathered[...].reshape(sources, slots)), 1)
-    value = product(
-        [(weights[:, n : n + 256], right[n : n + 256]) for n in range(0, sources, 256)]
-    )
-    value = value[: 8 * count_x] + value[8 * count_x :]
+    high, low = two_parts(gathered[...].reshape(2 * count_z * 8, slots))
+    both = jnp.concatenate([high, low], 1)
+    both = jnp.concatenate([both, both], 0)
+    half = weight_rows.shape[0] // 2
+    values = products([[(weight_rows[pl.ds(n * half, half), :], both)] for n in range(2)])
+    value = jnp.concatenate(values, 0)
     value = value[:, :slots] + value[:, slots:]
-    partial[...] = value.reshape(count_x, 8, slots)
-    copies_x = [line_copy(0, u, partial.at[u], received.at[u]) for u in range(1, count_x)]
-    for copy in copies_x:
+    partial[...] = value.reshape(count_x, chips, 8, slots)
+    copies_out = [
+        pltpu.make_async_remote_copy(
+            src_ref=partial.at[u, v],
+            dst_ref=received.at[u, v],
+            send_sem=reduce_send.at[u, v],
+            recv_sem=reduce_recv.at[u, v],
+            device_id=device(u, 2 * v, 0),
+            device_id_type=MESH,
+        )
+        for u, v in goals
+    ]
+    for copy in copies_out:
         copy.start()
 
     for copy in copies_halo:
@@ -477,33 +536,35 @@
         second = row(near_c, 36 + c) - sum(position[b] * row(near_c, 3 * b + c) for b in range(3))
         near.append(near_scale * (first - position[c] * still + second))
 
-    for copy in copies_x:
+    for copy in copies_out:
         copy.wait()
-    summed_moments = partial[0]
-    for u in range(1, count_x):
-        summed_moments = summed_moments + received[u]
+    received[0, 0] = partial[0, 0]
+    summed_moments = jnp.sum(received[...].reshape(count_x * chips, 8, slots), 0)
     high, low = high_low(summed_moments)
     left = jnp.concatenate([high, low], 0).astype(bf16)
     left = jnp.concatenate([left, jnp.zeros((16, slots), bf16)], 1)
-    highs, lows = [], []
+    groups = []
     for m in range(3):
         right = translation_rows[:, pl.ds(2 * m * slots, 2 * slots)]
-        right = jnp.concatenate([right, jnp.zeros((slots, 2 * slots), bf16)], 0)
-        value = product([(left, right)], m % 2)
+        groups.append([(left, jnp.concatenate([right, jnp.zeros((slots, 2 * slots), bf16)], 0))])
+    highs, lows = [], []
+    for value in products(groups):
         value = value[:8] + value[8:]
         value = value[:, :slots] + value[:, slots:]
         for part, result in zip(high_low(value), (highs, lows)):
             result.append(part + pltpu.roll(part, term_rows, 1))
     left = [jnp.concatenate(parts + [zero], 0).astype(bf16) for parts in (highs, lows)]
     left = jnp.concatenate(left, 1)
-    far = [zero] * 3
+    groups = []
     for first in range(0, 8, 2):
         right = jnp.concatenate([poly_rows[first], poly_rows[first + 1]], 1)
-        fields = product([(left, jnp.concatenate([right, right], 0))], first // 2 % 2)
+        groups.append([(left, jnp.concatenate([right, right], 0))])
+    far = [zero] * 3
+    for pair, fields in enumerate(products(groups)):
         for m in range(3):
             for n in range(2):
                 field = fields[8 * m : 8 * m + 8, n * slots : (n + 1) * slots]
-                far[m] = jnp.where(cell == first + n, field, far[m])
+                far[m] = jnp.where(cell == 2 * pair + n, field, far[m])
     far = [value * mask for value in far]
 
     stressed = [sum(stress_ref[a, b] * charge[b] for b in range(3)) for a in range(3)]
@@ -517,20 +578,28 @@
 
 
 def body(sizes, offsets, lines, burgers, counts, mobility, stress, translation):
-    vmem, smem = (pl.BlockSpec(memory_space=space) for space in (pltpu.VMEM, pltpu.SMEM))
+    vmem, hbm = (pl.BlockSpec(memory_space=space) for space in (pltpu.VMEM, pltpu.HBM))
     shape = offsets.shape
     flat = (3, 8, slots)
-    longest = max(sizes)
+    chips = sizes[1] // 2
     result = pl.pallas_call(
         functools.partial(kernel, sizes),
         out_shape=jax.ShapeDtypeStruct(flat, f32),
-        in_specs=[vmem, vmem, vmem, smem, smem, smem, vmem],
+        in_specs=[hbm] * 7,
         out_specs=vmem,
         scratch_shapes=[
+            pltpu.VMEM(flat, f32),
+            pltpu.VMEM(flat, f32),
+            pltpu.VMEM(flat, f32),
+            pltpu.SMEM(counts.shape, jnp.int32),
+            pltpu.SMEM(mobility.shape, f32),
+            pltpu.SMEM(stress.shape, f32),
+            pltpu.VMEM(translation.shape, f32),
+            pltpu.SemaphoreType.DMA((7,)),
             pltpu.VMEM((4, 4, 4, 16, slots), f32),
-            pltpu.VMEM((sizes[1], sizes[2], 8, slots), f32),
-            pltpu.VMEM((sizes[0], 8, slots), f32),
-            pltpu.VMEM((sizes[0], 8, slots), f32),
+            pltpu.VMEM((2, sizes[2], 8, slots), f32),
+            pltpu.VMEM((sizes[0], chips, 8, slots), f32),
+            pltpu.VMEM((sizes[0], chips, 8, slots), f32),
             pltpu.VMEM((8 * source_rows, slots), f32),
             pltpu.VMEM((8 * split_rows, slots), f32),
             pltpu.VMEM((8 * term_rows, slots), f32),
@@ -541,17 +610,20 @@
             pltpu.VMEM((8, 4, 4 * split_rows, 2 * slots), bf16),
             pltpu.VMEM((8, slots, slots), bf16),
             pltpu.VMEM((slots, 6 * slots), bf16),
+            pltpu.VMEM((sizes[0] * chips * 8, 4 * sizes[2] * 8), bf16),
             pltpu.VMEM((8 * source_rows, slots), f32),
             pltpu.VMEM((8 * source_rows, slots), f32),
             pltpu.VMEM((8 * source_rows, slots), f32),
             pltpu.VMEM((8 * source_rows, slots), f32),
             pltpu.SemaphoreType.DMA((26,)),
             pltpu.SemaphoreType.DMA((26,)),
-            pltpu.SemaphoreType.DMA((3, longest)),
-            pltpu.SemaphoreType.DMA((3, longest)),
+            pltpu.SemaphoreType.DMA((2, sizes[2])),
+            pltpu.SemaphoreType.DMA((2, sizes[2])),
+            pltpu.SemaphoreType.DMA((sizes[0], chips)),
+            pltpu.SemaphoreType.DMA((sizes[0], chips)),
         ],
         compiler_params=pltpu.CompilerParams(
-            collective_id=0, has_side_effects=True, vmem_limit_bytes=48 * 1024 * 1024
+            collective_id=0, has_side_effects=True, vmem_limit_bytes=60 * 1024 * 1024
         ),
     )(
         offsets.reshape(flat),

time: 41.6 us -> 37.5 us (0.901)
  local copies, waits for them, and re-layouts: 4.94 us -> 1.31 us
    unnamed x15 -> x1, local copies, waits for them, and re-layouts: 4.94 us -> 1.31 us
where the time goes in v3:
time: 37.5 us; the launch traced here: 37.3 us
  Pallas kernels  36 us (96%)
  local copies, waits for them, and re-layouts  1.31 us (3%)
    pallas_call x1, Pallas kernels, body(): pl.pallas_call(functools.partial(kernel, sizes), out_shape=jax.ShapeDtype...  36 us
    unnamed x1, local copies, waits for them, and re-layouts  1.31 us

profile of v3, /device:TPU:1, one launch (start us, length us, event | category | flops | bytes accessed | tf_op | source)
XLA Modules:
  0.0 37.3 jit_solution(9197942208509829665)
XLA Ops:
  0.0 36.0 %shard_map.73 = f32[3,8,128]{2,1,0:T(8,128)} custom-call(f32[3,8,128]{2,1,0:T(8,128)} %bitcast.5, f32[3,8,128]{2,1,0:T(8,128)} %bitcast.6, f32[3,8,128]{2,1,0:T(8,128)} %bitcast.7, s32[2,2,2]{2,1,0:T(2,128)} %counts_in.1, f32[2,2,2]{2,1,0:T(2,128)} %mobility_in.1, f32[3,3]{1,0:T(4,128)} %stress_in.1, f32[128,128]{1,0:T(8,128)} %translation_in.1), custom_call_target="tpu_custom_call" | custom-call | tf_op jit(solution)/shard_map/pallas_call | solution.py:585
  36.0 1.3 %copy.9 = f32[3,2,2,2,128]{4,3,2,1,0:T(2,128)} copy(f32[3,2,2,2,128]{4,3,2,1,0:T(2,128)} %bitcast.4) | data formatting | bytes 24576

commit v4 on v3

--- a/solution.py
+++ b/solution.py
@@ -104,17 +104,17 @@
     return flat[pl.ds(group * 8 * 16 + n, 8, stride=16), :]
 
 
-def pack_sources(stage_rows, stage_split, out_rows, out_split, first, first_split):
+def pack_sources(stage_rows, stage_split, out_rows, out_split, first, first_split, part=0):
     zero = jnp.zeros((source_rows, slots), f32)
     for cell in range(8):
-        value = stage_rows[pl.ds(cell * source_rows, source_rows), :]
+        value = stage_rows[pl.ds((8 * part + cell) * source_rows, source_rows), :]
         high, low = high_low(value)
         out_rows[first + cell, :, pl.ds(0, slots)] = jnp.concatenate([high, low], 0).astype(bf16)
         out_rows[first + cell, :, pl.ds(slots, slots)] = jnp.concatenate([high, zero], 0).astype(
             bf16
         )
     for half in range(2):
-        value = stage_split[pl.ds(half * 4 * split_rows, 4 * split_rows), :]
+        value = stage_split[pl.ds((2 * part + half) * 4 * split_rows, 4 * split_rows), :]
         out_split[first_split + half] = value.T.astype(bf16)
 
 
@@ -401,8 +401,8 @@
     }
     copies_halo = []
     for n, step in enumerate(offsets_26):
-        source = tuple(sides[s][0] for s in step)
-        target = tuple(sides[s][1] for s in step)
+        source = tuple(sides[s][0] for s in step) + (pl.ds(0, 9),)
+        target = tuple(sides[s][1] for s in step) + (pl.ds(0, 9),)
         copies_halo.append(
             pltpu.make_async_remote_copy(
                 src_ref=halo.at[source],
@@ -504,23 +504,27 @@
     for copy in copies_halo:
         copy.wait()
 
-    def prepare(group, _):
-        value = [eight_cells(halo, group, n) for n in range(9)]
-        place = [
-            jnp.zeros((8, slots), jnp.int32) + group // 2,
-            group % 2 * 2 + cell // 4,
-            cell % 4,
-        ]
-        position = [value[c] + (place[c].astype(f32) - 1.5) for c in range(3)]
-        rows, splits = source_values(position, value[3:6], value[6:9])
-        store_rows(stage_rows, rows, source_rows)
-        store_rows(stage_split, splits, split_rows)
-        pack_sources(
-            stage_rows, stage_split, halo_rows, halo_split, group * 8, group * 2
-        )
+    def prepare(pair, _):
+        for half in range(2):
+            group = 2 * pair + half
+            value = [eight_cells(halo, group, n) for n in range(9)]
+            place = [
+                jnp.zeros((8, slots), jnp.int32) + pair,
+                2 * half + cell // 4,
+                cell % 4,
+            ]
+            position = [value[c] + (place[c].astype(f32) - 1.5) for c in range(3)]
+            rows, splits = source_values(position, value[3:6], value[6:9])
+            store_rows(stage_rows, rows, source_rows, 8 * source_rows * half)
+            store_rows(stage_split, splits, split_rows, 8 * split_rows * half)
+        for half in range(2):
+            group = 2 * pair + half
+            pack_sources(
+                stage_rows, stage_split, halo_rows, halo_split, group * 8, group * 2, half
+            )
         return 0
 
-    lax.fori_loop(0, 8, prepare, 0)
+    lax.fori_loop(0, 4, prepare, 0)
     near_halo()
 
     def row(refs, n):
@@ -535,6 +539,12 @@
         first = sum(pairs[n] * row(near_w, 9 + 9 * c + n) for n in range(9))
         second = row(near_c, 36 + c) - sum(position[b] * row(near_c, 3 * b + c) for b in range(3))
         near.append(near_scale * (first - position[c] * still + second))
+
+    stressed = [sum(stress_ref[a, b] * charge[b] for b in range(3)) for a in range(3)]
+    applied = crossed(stressed, lines)
+    known = [near[c] + applied[c] for c in range(3)]
+    shorten = 1.0 / jnp.maximum(sum(lines[c] * lines[c] for c in range(3)), 1.0)
+    scale = mobility * mask
 
     for copy in copies_out:
         copy.wait()
@@ -567,12 +577,9 @@
                 far[m] = jnp.where(cell == 2 * pair + n, field, far[m])
     far = [value * mask for value in far]
 
-    stressed = [sum(stress_ref[a, b] * charge[b] for b in range(3)) for a in range(3)]
-    applied = crossed(stressed, lines)
-    force = [near[c] + far[c] + applied[c] for c in range(3)]
+    force = [known[c] + far[c] for c in range(3)]
     along = sum(force[c] * lines[c] for c in range(3))
-    along = along / jnp.maximum(sum(lines[c] * lines[c] for c in range(3)), 1.0)
-    scale = mobility * mask
+    along = along * shorten
     for c in range(3):
         out_ref[c] = scale * (force[c] - along * lines[c])
 
@@ -600,8 +607,8 @@
             pltpu.VMEM((2, sizes[2], 8, slots), f32),
             pltpu.VMEM((sizes[0], chips, 8, slots), f32),
             pltpu.VMEM((sizes[0], chips, 8, slots), f32),
-            pltpu.VMEM((8 * source_rows, slots), f32),
-            pltpu.VMEM((8 * split_rows, slots), f32),
+            pltpu.VMEM((16 * source_rows, slots), f32),
+            pltpu.VMEM((16 * split_rows, slots), f32),
             pltpu.VMEM((8 * term_rows, slots), f32),
             pltpu.VMEM((8, 2 * source_rows, 2 * slots), bf16),
             pltpu.VMEM((2, slots, 4 * split_rows), bf16),

time: 37.5 us -> 35.8 us (0.955)
  Pallas kernels: 36 us -> 34.3 us
    pallas_call x1, Pallas kernels: 36 us -> 34.3 us  [body(): pl.pallas_call(functools.partial(kernel, sizes), out_shape=jax.ShapeDtype...]
where the time goes in v4:
time: 35.8 us; the launch traced here: 35.7 us
  Pallas kernels  34.3 us (96%)
  local copies, waits for them, and re-layouts  1.31 us (4%)
    pallas_call x1, Pallas kernels, body(): pl.pallas_call(functools.partial(kernel, sizes), out_shape=jax.ShapeDtype...  34.3 us
    unnamed x1, local copies, waits for them, and re-layouts  1.31 us

profile of v4, /device:TPU:1, one launch (start us, length us, event | category | flops | bytes accessed | tf_op | source)
XLA Modules:
  0.0 35.7 jit_solution(6342624064180166524)
XLA Ops:
  0.0 34.3 %shard_map.73 = f32[3,8,128]{2,1,0:T(8,128)} custom-call(f32[3,8,128]{2,1,0:T(8,128)} %bitcast.5, f32[3,8,128]{2,1,0:T(8,128)} %bitcast.6, f32[3,8,128]{2,1,0:T(8,128)} %bitcast.7, s32[2,2,2]{2,1,0:T(2,128)} %counts_in.1, f32[2,2,2]{2,1,0:T(2,128)} %mobility_in.1, f32[3,3]{1,0:T(4,128)} %stress_in.1, f32[128,128]{1,0:T(8,128)} %translation_in.1), custom_call_target="tpu_custom_call" | custom-call | tf_op jit(solution)/shard_map/pallas_call | solution.py:592
  34.4 1.3 %copy.9 = f32[3,2,2,2,128]{4,3,2,1,0:T(2,128)} copy(f32[3,2,2,2,128]{4,3,2,1,0:T(2,128)} %bitcast.4) | data formatting | bytes 24576

commit v5 on v4

--- a/solution.py
+++ b/solution.py
@@ -140,7 +140,7 @@
 ahead = 4
 
 
-def near_sums(blocks, plan, target_rows, store):
+def near_sums(blocks, plan, target_rows, store, begin=0, end=8):
     count = len(blocks)
     held = next(n for n in range(ahead, 2 * ahead) if (count - ahead) % n == 0)
 
@@ -181,13 +181,13 @@
                 highs.append(high)
                 lows.append(low)
             if p == 0:
-                store(jnp.maximum(k - 1, 0), pltpu.matmul_pop(total))
+                store(jnp.maximum(k - 1, begin), pltpu.matmul_pop(total))
             _, _, _, rows, place = plan(k, p)
             pltpu.matmul_push_rhs(jnp.concatenate(highs + lows, 0), p % 2, 1)
             pltpu.matmul_acc_lhs(total, rows[place], load_staged_rhs=p % 2)
 
         def target(k, _):
-            after = jnp.minimum(k + 1, 7)
+            after = jnp.minimum(k + 1, end - 1)
             for p in range(count):
                 finish(p, k)
                 if p + ahead < count:
@@ -196,11 +196,11 @@
                     start(p + ahead - count, after, after)
             return 0
 
-        stage(0, 0)
+        stage(0, begin)
         for p in range(ahead):
-            start(p, 0, 1)
-        lax.fori_loop(0, 8, target, 0)
-        store(7, pltpu.matmul_pop(total))
+            start(p, begin, begin)
+        lax.fori_loop(begin, end, target, 0)
+        store(end - 1, pltpu.matmul_pop(total))
         pltpu.matmul_acc_lhs(
             buffer(0, 0), jnp.zeros((chunk, 2 * slots), bf16), load_staged_rhs=0
         )
@@ -296,24 +296,6 @@
     for step in partners:
         pl.semaphore_signal(barrier, inc=1, device_id=device(*step), device_id_type=MESH)
 
-    shape = (count_x * chips * 8, 2 * count_z * 8)
-    goal = lax.broadcasted_iota(jnp.int32, shape, 0)
-    source = lax.broadcasted_iota(jnp.int32, shape, 1)
-    apart = [
-        2 * (goal // (8 * chips)) + goal // 4 % 2 - source // 4 % 2,
-        4 * (goal // 8 % chips) - 2 * over * (source // (8 * count_z)) + goal // 2 % 2 - source // 2 % 2,
-        2 * (source // 8 % count_z) + goal % 2 - source % 2,
-    ]
-    largest, total_sq = 0, 0
-    for axis in range(3):
-        extent = 2 * sizes[axis]
-        steps = lax.rem(apart[axis] + extent, extent)
-        steps = jnp.minimum(steps, extent - steps)
-        largest = jnp.maximum(largest, steps)
-        total_sq = total_sq + steps * steps
-    weights = jnp.where(largest > 1, lax.rsqrt(jnp.maximum(total_sq, 1).astype(f32)), 0.0)
-    weight_rows[...] = jnp.concatenate(two_parts(weights), 1)
-
     target_rows[...] = jnp.zeros(target_rows.shape, bf16)
 
     for load in loads[:4]:
@@ -453,15 +435,34 @@
         z = (1, 2, 3 * (k % 2))[z]
         return z, halo_split, 4 * x + y, halo_rows, 16 * x + 4 * y + z
 
-    def near_local():
+    def near_local(begin, end):
         blocks = [source % 4 for source in local_order]
-        near_sums(blocks, local_plan, target_rows, functools.partial(keep, near_w, near_c))
+        keep_local = functools.partial(keep, near_w, near_c)
+        near_sums(blocks, local_plan, target_rows, keep_local, begin, end)
 
     def near_halo():
         blocks = [z for _, z in halo_order]
         near_sums(blocks, halo_plan, target_rows, functools.partial(keep, halo_w, halo_c))
 
-    near_local()
+    shape = (count_x * chips * 8, 2 * count_z * 8)
+    goal = lax.broadcasted_iota(jnp.int32, shape, 0)
+    source = lax.broadcasted_iota(jnp.int32, shape, 1)
+    apart = [
+        2 * (goal // (8 * chips)) + goal // 4 % 2 - source // 4 % 2,
+        4 * (goal // 8 % chips) - 2 * over * (source // (8 * count_z)) + goal // 2 % 2 - source // 2 % 2,
+        2 * (source // 8 % count_z) + goal % 2 - source % 2,
+    ]
+    largest, total_sq = 0, 0
+    for axis in range(3):
+        extent = 2 * sizes[axis]
+        steps = lax.rem(apart[axis] + extent, extent)
+        steps = jnp.minimum(steps, extent - steps)
+        largest = jnp.maximum(largest, steps)
+        total_sq = total_sq + steps * steps
+    weights = jnp.where(largest > 1, lax.rsqrt(jnp.maximum(total_sq, 1).astype(f32)), 0.0)
+    weight_rows[...] = jnp.concatenate(two_parts(weights), 1)
+
+    near_local(0, 8)
     for load in loads[4:]:
         load.wait()
     mobility = jnp.zeros((8, slots), f32)
@@ -591,7 +592,7 @@
     chips = sizes[1] // 2
     result = pl.pallas_call(
         functools.partial(kernel, sizes),
-        out_shape=jax.ShapeDtypeStruct(flat, f32),
+        out_shape=pltpu.VMEM(flat, f32),
         in_specs=[hbm] * 7,
         out_specs=vmem,
         scratch_shapes=[

time: 35.8 us -> 34.5 us (0.964)
  local copies, waits for them, and re-layouts: 1.31 us -> 0.6 us
  Pallas kernels: 34.3 us -> 33.8 us
    unnamed x1, local copies, waits for them, and re-layouts: 1.31 us -> 0.6 us
    pallas_call x1, Pallas kernels: 34.3 us -> 33.8 us  [body(): pl.pallas_call(functools.partial(kernel, sizes), out_shape=pltpu.VMEM(fla...]
where the time goes in v5:
time: 34.5 us; the launch traced here: 34.4 us
  Pallas kernels  33.8 us (98%)
  local copies, waits for them, and re-layouts  0.6 us (2%)
    pallas_call x1, Pallas kernels, body(): pl.pallas_call(functools.partial(kernel, sizes), out_shape=pltpu.VMEM(fla...  33.8 us

profile of v5, /device:TPU:1, one launch (start us, length us, event | category | flops | bytes accessed | tf_op | source)
XLA Modules:
  0.0 34.4 jit_solution(8646396073511232637)
XLA Ops:
  0.0 33.8 %shard_map.73 = f32[3,8,128]{2,1,0:T(8,128)S(1)} custom-call(f32[3,8,128]{2,1,0:T(8,128)} %bitcast.5, f32[3,8,128]{2,1,0:T(8,128)} %bitcast.6, f32[3,8,128]{2,1,0:T(8,128)} %bitcast.7, s32[2,2,2]{2,1,0:T(2,128)} %counts_in.1, f32[2,2,2]{2,1,0:T(2,128)} %mobility_in.1, f32[3,3]{1,0:T(4,128)} %stress_in.1, f32[128,128]{1,0:T(8,128)} %translation_in.1), custom_call_target="tpu_custom_call" | custom-call | tf_op jit(solution)/shard_map/pallas_call | solution.py:593
  33.8 0.6 %copy.9 = f32[3,2,2,2,128]{4,3,2,1,0:T(2,128)} copy(f32[3,2,2,2,128]{4,3,2,1,0:T(2,128)S(1)} %bitcast.4) | data formatting | bytes 24576

commit v6 on v4

--- a/solution.py
+++ b/solution.py
@@ -137,12 +137,12 @@
 
 chunk = 32
 chunks = slots // chunk
-ahead = 4
-
-
-def near_sums(blocks, plan, target_rows, store):
+ahead = 3
+
+
+def near_sums(blocks, plan, target_rows, store, begin=0, end=8):
     count = len(blocks)
-    held = next(n for n in range(ahead, 2 * ahead) if (count - ahead) % n == 0)
+    held = ahead + 1
 
     def scope(total, *buffers):
         def buffer(p, n):
@@ -181,13 +181,13 @@
                 highs.append(high)
                 lows.append(low)
             if p == 0:
-                store(jnp.maximum(k - 1, 0), pltpu.matmul_pop(total))
+                store(jnp.maximum(k - 1, begin), pltpu.matmul_pop(total))
             _, _, _, rows, place = plan(k, p)
             pltpu.matmul_push_rhs(jnp.concatenate(highs + lows, 0), p % 2, 1)
             pltpu.matmul_acc_lhs(total, rows[place], load_staged_rhs=p % 2)
 
         def target(k, _):
-            after = jnp.minimum(k + 1, 7)
+            after = jnp.minimum(k + 1, end - 1)
             for p in range(count):
                 finish(p, k)
                 if p + ahead < count:
@@ -196,11 +196,11 @@
                     start(p + ahead - count, after, after)
             return 0
 
-        stage(0, 0)
+        stage(0, begin)
         for p in range(ahead):
-            start(p, 0, 1)
-        lax.fori_loop(0, 8, target, 0)
-        store(7, pltpu.matmul_pop(total))
+            start(p, begin, begin)
+        lax.fori_loop(begin, end, target, 0)
+        store(end - 1, pltpu.matmul_pop(total))
         pltpu.matmul_acc_lhs(
             buffer(0, 0), jnp.zeros((chunk, 2 * slots), bf16), load_staged_rhs=0
         )
@@ -453,15 +453,16 @@
         z = (1, 2, 3 * (k % 2))[z]
         return z, halo_split, 4 * x + y, halo_rows, 16 * x + 4 * y + z
 
-    def near_local():
+    def near_local(begin, end):
         blocks = [source % 4 for source in local_order]
-        near_sums(blocks, local_plan, target_rows, functools.partial(keep, near_w, near_c))
+        keep_local = functools.partial(keep, near_w, near_c)
+        near_sums(blocks, local_plan, target_rows, keep_local, begin, end)
 
     def near_halo():
         blocks = [z for _, z in halo_order]
         near_sums(blocks, halo_plan, target_rows, functools.partial(keep, halo_w, halo_c))
 
-    near_local()
+    near_local(0, 8)
     for load in loads[4:]:
         load.wait()
     mobility = jnp.zeros((8, slots), f32)
@@ -504,27 +505,27 @@
     for copy in copies_halo:
         copy.wait()
 
-    def prepare(pair, _):
-        for half in range(2):
-            group = 2 * pair + half
+    def prepare(planes, _):
+        for part in range(4):
+            group = 4 * planes + part
             value = [eight_cells(halo, group, n) for n in range(9)]
             place = [
-                jnp.zeros((8, slots), jnp.int32) + pair,
-                2 * half + cell // 4,
+                jnp.zeros((8, slots), jnp.int32) + 2 * planes + part // 2,
+                part % 2 * 2 + cell // 4,
                 cell % 4,
             ]
             position = [value[c] + (place[c].astype(f32) - 1.5) for c in range(3)]
             rows, splits = source_values(position, value[3:6], value[6:9])
-            store_rows(stage_rows, rows, source_rows, 8 * source_rows * half)
-            store_rows(stage_split, splits, split_rows, 8 * split_rows * half)
-        for half in range(2):
-            group = 2 * pair + half
+            store_rows(stage_rows, rows, source_rows, 8 * source_rows * part)
+            store_rows(stage_split, splits, split_rows, 8 * split_rows * part)
+        for part in range(4):
+            group = 4 * planes + part
             pack_sources(
-                stage_rows, stage_split, halo_rows, halo_split, group * 8, group * 2, half
+                stage_rows, stage_split, halo_rows, halo_split, group * 8, group * 2, part
             )
         return 0
 
-    lax.fori_loop(0, 4, prepare, 0)
+    lax.fori_loop(0, 2, prepare, 0)
     near_halo()
 
     def row(refs, n):
@@ -591,7 +592,7 @@
     chips = sizes[1] // 2
     result = pl.pallas_call(
         functools.partial(kernel, sizes),
-        out_shape=jax.ShapeDtypeStruct(flat, f32),
+        out_shape=pltpu.VMEM(flat, f32),
         in_specs=[hbm] * 7,
         out_specs=vmem,
         scratch_shapes=[
@@ -607,8 +608,8 @@
             pltpu.VMEM((2, sizes[2], 8, slots), f32),
             pltpu.VMEM((sizes[0], chips, 8, slots), f32),
             pltpu.VMEM((sizes[0], chips, 8, slots), f32),
-            pltpu.VMEM((16 * source_rows, slots), f32),
-            pltpu.VMEM((16 * split_rows, slots), f32),
+            pltpu.VMEM((32 * source_rows, slots), f32),
+            pltpu.VMEM((32 * split_rows, slots), f32),
             pltpu.VMEM((8 * term_rows, slots), f32),
             pltpu.VMEM((8, 2 * source_rows, 2 * slots), bf16),
             pltpu.VMEM((2, slots, 4 * split_rows), bf16),

time: 35.8 us -> 34.1 us (0.953)
  Pallas kernels: 34.3 us -> 33.4 us
  local copies, waits for them, and re-layouts: 1.31 us -> 0.6 us
    pallas_call x1, Pallas kernels: 34.3 us -> 33.4 us  [body(): pl.pallas_call(functools.partial(kernel, sizes), out_shape=pltpu.VMEM(fla...]
    unnamed x1, local copies, waits for them, and re-layouts: 1.31 us -> 0.6 us
where the time goes in v6:
time: 34.1 us; the launch traced here: 34 us
  Pallas kernels  33.4 us (98%)
  local copies, waits for them, and re-layouts  0.6 us (2%)
    pallas_call x1, Pallas kernels, body(): pl.pallas_call(functools.partial(kernel, sizes), out_shape=pltpu.VMEM(fla...  33.4 us

profile of v6, /device:TPU:1, one launch (start us, length us, event | category | flops | bytes accessed | tf_op | source)
XLA Modules:
  0.0 34.0 jit_solution(10427459294454171072)
XLA Ops:
  0.0 33.4 %shard_map.73 = f32[3,8,128]{2,1,0:T(8,128)S(1)} custom-call(f32[3,8,128]{2,1,0:T(8,128)} %bitcast.5, f32[3,8,128]{2,1,0:T(8,128)} %bitcast.6, f32[3,8,128]{2,1,0:T(8,128)} %bitcast.7, s32[2,2,2]{2,1,0:T(2,128)} %counts_in.1, f32[2,2,2]{2,1,0:T(2,128)} %mobility_in.1, f32[3,3]{1,0:T(4,128)} %stress_in.1, f32[128,128]{1,0:T(8,128)} %translation_in.1), custom_call_target="tpu_custom_call" | custom-call | tf_op jit(solution)/shard_map/pallas_call | solution.py:593
  33.4 0.6 %copy.9 = f32[3,2,2,2,128]{4,3,2,1,0:T(2,128)} copy(f32[3,2,2,2,128]{4,3,2,1,0:T(2,128)S(1)} %bitcast.4) | data formatting | bytes 24576

commit v7 on v6

--- a/solution.py
+++ b/solution.py
@@ -373,12 +373,6 @@
         total = total + (part if m == 0 else pltpu.roll(part, terms * m, 1))
     gathered[0, 0] = total * (1.0 / slots)
 
-    for c in range(3):
-        for first, value in ((0, offsets), (3, lines), (6, charge)):
-            for k in range(8):
-                where = (1 + k // 4, 1 + k // 2 % 2, 1 + k % 2, pl.ds(first + c, 1))
-                halo[where] = value[c][k : k + 1]
-
     pl.semaphore_wait(barrier, len(partners))
 
     copies_in = [
@@ -394,6 +388,13 @@
     ]
     for copy in copies_in:
         copy.start()
+
+    for c in range(3):
+        for first, value in ((0, offsets), (3, lines), (6, charge)):
+            for k in range(8):
+                where = (1 + k // 4, 1 + k // 2 % 2, 1 + k % 2, pl.ds(first + c, 1))
+                halo[where] = value[c][k : k + 1]
+
     sides = {
         -1: (pl.ds(1, 1), pl.ds(3, 1)),
         0: (pl.ds(1, 2), pl.ds(1, 2)),

time: 34.1 us -> 34.1 us (level)
  no operation moved by 1% of the time
where the time goes in v7:
time: 34.1 us; the launch traced here: 34 us
  Pallas kernels  33.4 us (98%)
  local copies, waits for them, and re-layouts  0.6 us (2%)
    pallas_call x1, Pallas kernels, body(): pl.pallas_call(functools.partial(kernel, sizes), out_shape=pltpu.VMEM(fla...  33.4 us

profile of v7, /device:TPU:1, one launch (start us, length us, event | category | flops | bytes accessed | tf_op | source)
XLA Modules:
  0.0 34.0 jit_solution(4246188819605213860)
XLA Ops:
  0.0 33.4 %shard_map.73 = f32[3,8,128]{2,1,0:T(8,128)S(1)} custom-call(f32[3,8,128]{2,1,0:T(8,128)} %bitcast.5, f32[3,8,128]{2,1,0:T(8,128)} %bitcast.6, f32[3,8,128]{2,1,0:T(8,128)} %bitcast.7, s32[2,2,2]{2,1,0:T(2,128)} %counts_in.1, f32[2,2,2]{2,1,0:T(2,128)} %mobility_in.1, f32[3,3]{1,0:T(4,128)} %stress_in.1, f32[128,128]{1,0:T(8,128)} %translation_in.1), custom_call_target="tpu_custom_call" | custom-call | tf_op jit(solution)/shard_map/pallas_call | solution.py:594
  33.4 0.6 %copy.9 = f32[3,2,2,2,128]{4,3,2,1,0:T(2,128)} copy(f32[3,2,2,2,128]{4,3,2,1,0:T(2,128)S(1)} %bitcast.4) | data formatting | bytes 24576
